TPU v7x, 128 devices: a whole 4x4x4 slice. The times are simulated.
128 devices in a mesh: dp: 32 (over x, y, core), ctx: 4 (over z).
Axes of the slice: x: 4, y: 4, z: 4, core: 2. Of those that a mesh axis runs over, the one named last changes fastest.
Arguments:
- tokens: bfloat16 [32768, 1024], P(('dp', 'ctx')), may hold values from -6 to 6
- send_rows: int32 [128, 256], P(('dp', 'ctx')), may hold values from 0 to 255, each once within a row
- user_lengths: int32 [32, 3], P('dp'), may hold values from 1 to 512, 1024 in all within a row
- input_weight: bfloat16 [1024, 4096], replicated, may hold values from -0.1875 to 0.1875
- output_weight: bfloat16 [1024, 1024], replicated, may hold values from -0.1875 to 0.1875
- distance_bias: float32 [8, 12], replicated, may hold values from 0.5 to 2.5
- upstream: bfloat16 [32768, 1024], P(('dp', 'ctx')), may hold values from -6 to 6
Outputs:
- layer_output: bfloat16 [32768, 1024], P(('dp', 'ctx'))
- token_gradient: bfloat16 [32768, 1024], P(('dp', 'ctx'))
- input_gradient: float32 [1024, 4096], P(('dp', 'ctx'))
- output_gradient: float32 [1024, 1024], P(('dp', 'ctx'))
- bias_gradient: float32 [8, 12], replicated
Inputs may be any that keep to these rules, and one draw needn't show every extreme that they name: Each device's row of send_rows is a permutation of its 256 local rows; entry j names the row that goes to dp index j // 8, into slot j % 8. `user_lengths`: row d holds the history lengths of the 3 users of dp index d in buffer order; they sum to 1024 and the longest is 512.
All inputs are finite; a program needn't handle non-finite values.
Results may differ from a plain program's by a relative error of at most 0.0095.
Values may be sent and summed in bfloat16 or wider, within the bound.
A program may use at most 192 MiB of HBM per device.

v0:
```python
import jax
import jax.numpy as jnp
from jax import lax
from jax.sharding import PartitionSpec as P

H = 8
DH = 128
NB = 12


EPSILON = 1e-05
HIGHEST = lax.Precision.HIGHEST


def layer_norm(values):
    row_mean = jnp.mean(values, axis=-1, keepdims=True)
    centered = values - row_mean
    inverse = lax.rsqrt(jnp.mean(centered * centered, axis=-1, keepdims=True) + EPSILON)
    return (centered * inverse, inverse)


def norm_backward(unit_rows, inverse_rows, upstream_rows):
    mean_plain = jnp.mean(upstream_rows, axis=-1, keepdims=True)
    mean_cross = jnp.mean(upstream_rows * unit_rows, axis=-1, keepdims=True)
    return inverse_rows * (upstream_rows - mean_plain - unit_rows * mean_cross)


def silu_slope(values):
    logistic = jax.nn.sigmoid(values)
    return logistic * (1.0 + values * (1.0 - logistic))


def attention_pattern(query_index, key_index, lengths, bucket_count):
    user_ends = jnp.cumsum(lengths, dtype=jnp.int32)
    query_user = jnp.sum(
        (query_index[:, None] >= user_ends[None, :]).astype(jnp.int32), axis=1, dtype=jnp.int32
    )
    key_user = jnp.sum(
        (key_index[:, None] >= user_ends[None, :]).astype(jnp.int32), axis=1, dtype=jnp.int32
    )
    distance = query_index[:, None] - key_index[None, :]
    visible = jnp.logical_and(query_user[:, None] == key_user[None, :], distance >= 0).astype(
        jnp.float32
    )
    bucket = jnp.zeros(distance.shape, jnp.int32)
    for level_step in range(1, bucket_count):
        bucket = bucket + (distance + 1 >= 2**level_step).astype(jnp.int32)
    levels = jnp.arange(bucket_count, dtype=jnp.int32)
    onehot = (bucket[None, :, :] == levels[:, None, None]).astype(jnp.bfloat16)
    return (visible, onehot)


def bias_lookup(distance_bias, onehot):
    flat_table = onehot.reshape(onehot.shape[0], -1).astype(jnp.float32)
    flat_bias = jnp.dot(distance_bias, flat_table, precision=HIGHEST)
    return flat_bias.reshape((distance_bias.shape[0],) + onehot.shape[1:])


def bias_sums(score_gradient, onehot):
    flat_table = onehot.reshape(onehot.shape[0], -1).astype(jnp.float32)
    return lax.dot_general(
        score_gradient.reshape(score_gradient.shape[0], -1),
        flat_table,
        (((1,), (1,)), ((), ())),
        precision=HIGHEST,
    )


def row_products(left_rows, right_rows):
    return lax.dot_general(
        left_rows, right_rows, (((0,), (0,)), ((), ())), preferred_element_type=jnp.float32
    )


def shards(tokens, send_rows, user_lengths, input_weight, output_weight, distance_bias, upstream):
    row_count, model_width = tokens.shape
    group_count = lax.axis_size("dp")
    slot_count = row_count // group_count
    buffer_length = row_count * lax.axis_size("ctx")
    feature_width = H * DH
    score_scale = DH ** (-0.5)
    send_order = send_rows[0]
    lengths = user_lengths[0]
    ordered = jnp.take(tokens, send_order, axis=0).reshape(group_count, slot_count, model_width)
    balanced = lax.all_to_all(ordered, "dp", split_axis=0, concat_axis=0, tiled=True).reshape(
        row_count, model_width
    )
    features = balanced.astype(jnp.float32)
    unit_in, inverse_in = layer_norm(features)
    normed_in = unit_in.astype(jnp.bfloat16)
    projected = jnp.dot(normed_in, input_weight, preferred_element_type=jnp.float32)
    activated = jax.nn.silu(projected).astype(jnp.bfloat16)
    gate_part = activated[:, :feature_width]
    value_part = activated[:, feature_width : 2 * feature_width]
    query_part = activated[:, 2 * feature_width : 3 * feature_width]
    key_part = activated[:, 3 * feature_width :]
    all_keys, all_values = (
        lax.all_gather(key_part, "ctx", axis=0, tiled=True),
        lax.all_gather(value_part, "ctx", axis=0, tiled=True),
    )
    context_index = lax.axis_index("ctx")
    query_index = context_index * row_count + jnp.arange(row_count, dtype=jnp.int32)
    key_index = jnp.arange(buffer_length, dtype=jnp.int32)
    visible, onehot = attention_pattern(query_index, key_index, lengths, NB)
    query_heads = query_part.reshape(row_count, H, DH)
    key_heads = all_keys.reshape(buffer_length, H, DH)
    value_heads = all_values.reshape(buffer_length, H, DH)
    scores = (
        jnp.einsum("qhd,khd->hqk", query_heads, key_heads, preferred_element_type=jnp.float32)
        * score_scale
    )
    scores = scores + bias_lookup(distance_bias, onehot)
    weights = (jax.nn.silu(scores) * visible[None]).astype(jnp.bfloat16)
    attended = jnp.einsum("hqk,khd->qhd", weights, value_heads, preferred_element_type=jnp.float32)
    unit_out, inverse_out = layer_norm(attended.reshape(row_count, feature_width))
    gate_float = gate_part.astype(jnp.float32)
    gated_rows = (unit_out * gate_float).astype(jnp.bfloat16)
    layer_output = (
        features + jnp.dot(gated_rows, output_weight, preferred_element_type=jnp.float32)
    ).astype(jnp.bfloat16)
    gated_gradient = lax.dot_general(
        upstream, output_weight, (((1,), (1,)), ((), ())), preferred_element_type=jnp.float32
    )
    output_local = row_products(gated_rows, upstream)
    gate_gradient = gated_gradient * unit_out
    projected_slope = silu_slope(projected)
    attended_gradient = norm_backward(unit_out, inverse_out, gated_gradient * gate_float).astype(
        jnp.bfloat16
    )
    attended_heads = attended_gradient.reshape(row_count, H, DH)
    weight_gradient = jnp.einsum(
        "qhd,khd->hqk", attended_heads, value_heads, preferred_element_type=jnp.float32
    )
    score_gradient = weight_gradient * silu_slope(scores) * visible[None]
    bias_local = bias_sums(score_gradient, onehot)
    score_rounded = score_gradient.astype(jnp.bfloat16)
    query_gradient = jnp.einsum(
        "hqk,khd->qhd", score_rounded, key_heads, preferred_element_type=jnp.float32
    )
    query_gradient = query_gradient.reshape(row_count, feature_width) * score_scale
    row_total = lax.axis_size("ctx") * row_count
    key_block = jnp.einsum(
        "hqk,qhd->khd", score_rounded, query_heads, preferred_element_type=jnp.float32
    )
    value_block = jnp.einsum(
        "hqk,qhd->khd", weights, attended_heads, preferred_element_type=jnp.float32
    )
    key_sums = lax.psum_scatter(
        jnp.concatenate(
            (
                key_block.reshape(row_total, feature_width) * score_scale,
                value_block.reshape(row_total, feature_width),
            ),
            axis=1,
        ).astype(jnp.bfloat16),
        "ctx",
        scatter_dimension=0,
        tiled=True,
    ).astype(jnp.float32)
    key_gradient = key_sums[:, :feature_width]
    value_gradient = key_sums[:, feature_width:]
    joined = jnp.concatenate((gate_gradient, value_gradient, query_gradient, key_gradient), axis=1)
    projected_gradient = (joined * projected_slope).astype(jnp.bfloat16)
    input_gradient, output_gradient = (
        lax.psum_scatter(
            row_products(normed_in, projected_gradient),
            ("dp", "ctx"),
            scatter_dimension=0,
            tiled=True,
        ),
        lax.psum_scatter(output_local, ("dp", "ctx"), scatter_dimension=0, tiled=True),
    )
    bias_gradient = lax.psum(bias_local, ("dp", "ctx"))
    normed_gradient = lax.dot_general(
        projected_gradient,
        input_weight,
        (((1,), (1,)), ((), ())),
        preferred_element_type=jnp.float32,
    )
    balanced_gradient = (
        upstream.astype(jnp.float32) + norm_backward(unit_in, inverse_in, normed_gradient)
    ).astype(jnp.bfloat16)
    returned = lax.all_to_all(
        balanced_gradient.reshape(group_count, slot_count, model_width),
        "dp",
        split_axis=0,
        concat_axis=0,
        tiled=True,
    )
    token_gradient = (
        jnp.zeros_like(tokens).at[send_order].set(returned.reshape(row_count, model_width))
    )
    return (layer_output, token_gradient, input_gradient, output_gradient, bias_gradient)


def solution(mesh):
    in_specs = (
        P(("dp", "ctx"), None),
        P(("dp", "ctx"), None),
        P("dp", None),
        P(),
        P(),
        P(),
        P(("dp", "ctx"), None),
    )
    out_specs = (
        P(("dp", "ctx"), None),
        P(("dp", "ctx"), None),
        P(("dp", "ctx"), None),
        P(("dp", "ctx"), None),
        P(),
    )
    return jax.shard_map(shards, mesh=mesh, in_specs=in_specs, out_specs=out_specs, check_vma=False)
```

profile of v0, /device:TPU:0, one launch (start us, length us, event | category | flops | bytes accessed | tf_op | source)
XLA Modules:
  0.0 1515.1 jit_solution(3994644789527383727)
XLA Ops:
  7.2 0.8 compare_select_fusion.1
  8.1 0.5 broadcast.267
  8.6 1.3 reduce.8
  9.9 0.1 squeeze.6
  10.0 2.7 gather_fusion
  12.7 0.1 bitcast_select_fusion
  12.8 18.4 %all_to_all.10 = bf16[32,8,1024]{2,1,0:T(8,128)(2,1)S(1)} all-to-all(bf16[32,8,1024]{2,1,0:T(8,128)(2,1)S(1)} %bitcast_select_fusion), channel_id=1, replica_groups=mesh['dp'=32,'ctx'=4] {'dp'}, dimensions={0} | all-to-all | bytes 1048576 | tf_op jit(solution)/shard_map/all_to_all | solution.py:85
  31.2 0.1 convert_reduce_fusion
  31.4 0.1 div.37
  31.4 0.3 fusion.33
  31.7 0.1 rsqrt.20
  31.8 7.9 multiply_convert_fusion.2
  39.7 1.3 copy-done.8
  41.1 1.1 fusion.62
  42.2 0.0 all-gather.3.cloned.1.call-start
  42.3 0.1 iota_bitcast_fusion
  42.4 1.2 copy.59
  43.6 0.3 reduce-scatter.4.cloned.1.call-start
  43.9 0.9 sub.89
  44.9 3.4 convert_add_fusion.1
  48.2 0.2 reduce-window.8
  48.4 0.1 convert_reduce_fusion.1
  48.5 0.1 convert_reduce_fusion.2
  48.6 1.2 fusion.50
  49.8 10.2 fusion
  60.1 1.0 copy.55
  61.1 11.5 all-gather.5.cloned.1.call-done
  72.5 3.9 copy.56
  76.5 13.8 multiply_convert_fusion
  90.3 15.5 %all-gather.3.cloned.1.call-done = bf16[1024,1024]{1,0:T(8,128)(2,1)} async-done(((bf16[256,1024]{1,0:T(8,128)(2,1)}), bf16[1024,1024]{1,0:T(8,128)(2,1)}) %all-gather.3.cloned.1.call-update) | async-done | bytes 2097168 | tf_op jit(solution)/shard_map/all_gather | solution.py:99
  105.7 5.4 fusion.64
  111.1 2.6 copy.51
  113.8 1.5 fusion.35
  115.3 2.3 fusion.55
  117.6 2.9 multiply_convert_fusion.3
  120.5 2.0 copy.57
  122.5 4.4 convolution_convert_fusion
  127.0 3.9 copy.53
  130.9 7.9 multiply_multiply_fusion
  138.8 2.5 multiply_convert_fusion.1
  141.3 1.3 copy-done.1
  142.6 3.9 copy.52
  146.6 4.7 pad_maximum_fusion
  151.2 0.0 reduce-scatter.8.cloned.1.call-start
  151.3 3.7 fusion.65
  155.1 0.0 reduce-scatter.6.cloned.1.call-start
  155.1 6.6 fusion.14
  161.7 2.6 copy.54
  164.2 34.0 %reduce-scatter.4.cloned.1.call-done = bf16[256,2048]{1,0:T(8,128)(2,1)} async-done(((bf16[1024,2048]{1,0:T(8,128)(2,1)}), bf16[256,2048]{1,0:T(8,128)(2,1)}) %reduce-scatter.4.cloned.1.call-update) | async-done | bytes 1048592 | tf_op jit(solution)/shard_map/reduce_scatter | solution.py:148
  198.3 1.5 fusion.63
  199.8 0.3 copy-done.6
  200.2 3.2 fusion.5
  203.4 1.4 copy-done.3
  204.8 8.2 fusion.57
  213.0 2.2 convert_add_fusion
  215.2 6.6 fusion.61
  221.8 1.2 fusion.52
  223.0 7.4 all-to-all-start.1
  230.5 16.4 %fusion.19 = f32[8,12]{1,0:T(8,128)S(1)} fusion(s32[256,1024]{1,0:T(8,128)} %convert_add_fusion, f32[8,256,1024]{2,1,0:T(8,128)} %copy-done.1), kind=kOutput, calls=%fused_computation.37 | convolution fusion | flops 305135616 | bytes 9437568 | tf_op jit(solution)/shard_map/dot_general | solution.py:61
  246.9 66.5 %psum.7 = f32[8,12]{1,0:T(8,128)} all-reduce(f32[8,12]{1,0:T(8,128)S(1)} %fusion.19), channel_id=1, replica_groups=mesh['dp'=32,'ctx'=4] {'dp','ctx'}, use_global_device_ids=true, to_apply=%region_15.16 | all-reduce | flops 96 | bytes 768 | tf_op jit(solution)/shard_map/psum | solution.py:173
  313.4 1.5 fusion.18
  314.9 3.0 scatter_custom_fusion
  317.9 526.4 %reduce-scatter.8.cloned.1.call-done = f32[8,1024]{1,0:T(8,128)} async-done(((f32[1024,1024]{1,0:T(8,128)}), f32[8,1024]{1,0:T(8,128)}) %reduce-scatter.8.cloned.1.call-update) | async-done | bytes 32784 | tf_op jit(solution)/shard_map/reduce_scatter | solution.py:171
  844.2 664.1 %reduce-scatter.6.cloned.1.call-done = f32[8,4096]{1,0:T(8,128)} async-done(((f32[1024,4096]{1,0:T(8,128)}), f32[8,4096]{1,0:T(8,128)}) %reduce-scatter.6.cloned.1.call-update) | async-done | bytes 131088 | tf_op jit(solution)/shard_map/reduce_scatter | solution.py:165
  (39 shorter events, 0.3 us)
Async XLA Ops:
  7.2 108.1 %copy-start = (bf16[1024,1024]{1,0:T(8,128)(2,1)S(1)}, bf16[1024,1024]{1,0:T(8,128)(2,1)}, u32[]{:S(2)}) copy-start(bf16[1024,1024]{1,0:T(8,128)(2,1)} %param.11) | copy-start | bytes 6291460
  7.2 65.4 %all-gather.5.cloned.1.call-start = ((), (), s32[]{:S(2)}) async-start(), calls=%async_computation.6 | async-start | bytes 2621440 | tf_op jit(solution)/shard_map/all_gather | solution.py:98
  39.7 1.3 copy-start.8
  42.2 6.1 copy-start.12
  42.2 63.5 %all-gather.3.cloned.1.call-start = ((), (), s32[]{:S(2)}) async-start(), calls=%async_computation.5 | async-start | bytes 2621440 | tf_op jit(solution)/shard_map/all_gather | solution.py:99
  42.4 7.4 copy-start.11
  43.6 154.7 %reduce-scatter.4.cloned.1.call-start = ((), (), s32[]{:S(2)}) async-start(), calls=%async_computation.7 | async-start | bytes 5242880 | tf_op jit(solution)/shard_map/reduce_scatter | solution.py:148
  61.1 15.4 %copy-start.9 = (bf16[256,1024]{0,1:T(8,128)(2,1)S(1)}, bf16[256,1024]{0,1:T(8,128)(2,1)}, u32[]{:S(2)}) copy-start(bf16[256,1024]{0,1:T(8,128)(2,1)} %copy.55) | copy-start | bytes 1572868
  105.7 9.5 copy-start.4
  113.8 3.9 copy-start.2
  130.9 7.9 copy-start.10
  138.8 3.8 copy-start.1
  151.2 693.0 %reduce-scatter.8.cloned.1.call-start = ((), (), s32[]{:S(2)}) async-start(), calls=%async_computation.9 | async-start | bytes 4227072 | tf_op jit(solution)/shard_map/reduce_scatter | solution.py:171
  155.1 1353.3 %reduce-scatter.6.cloned.1.call-start = ((), (), s32[]{:S(2)}) async-start(), calls=%async_computation.8 | async-start | bytes 16908288 | tf_op jit(solution)/shard_map/reduce_scatter | solution.py:165
  198.3 1.5 copy-start.5
  198.3 1.9 copy-start.6
  203.4 1.4 copy-start.3
  223.0 91.9 %all-to-all-start.1 = ((bf16[32,8,1024]{2,1,0:T(8,128)(2,1)}), bf16[32,8,1024]{2,1,0:T(8,128)(2,1)}, u32[]{:S(2)}, u32[]{:S(2)}) async-start(bf16[32,8,1024]{2,1,0:T(8,128)(2,1)} %fusion.52), calls=%async_computation.2 | async-start | bytes 1048576 | tf_op jit(solution)/shard_map/all_to_all | solution.py:183
  230.5 82.9 %copy-start.7 = (bf16[256,1024]{1,0:T(8,128)(2,1)S(1)}, bf16[256,1024]{1,0:T(8,128)(2,1)}, u32[]{:S(2)}) copy-start(bf16[256,1024]{1,0:T(8,128)(2,1)} %get-tuple-element.10) | copy-start | bytes 1572868
Sparse Core Ops, SparseCore 0:
  42.3 30.1 all-gather.4
  74.8 30.9 all-gather.2
  151.4 46.8 reduce-scatter.3
  201.2 642.9 reduce-scatter.7
  847.0 661.2 reduce-scatter.5
where the time goes:
time: 1520 us
  waiting for transfers between devices  1250 us (82%)
  matrix products  97.4 us (6%)
  blocking collectives  84.9 us (6%)
  local copies, waits for them, and re-layouts  35.7 us (2%)
  other arithmetic  23.3 us (2%)
    reduce_scatter x1, waiting for transfers between devices, shards(): lax.psum_scatter(row_products(normed_in, projected_gradient), ('dp', 'ctx...  664 us
    reduce_scatter x1, waiting for transfers between devices, shards(): lax.psum_scatter(output_local, ('dp', 'ctx'), scatter_dimension=0, tiled=...  526 us
    psum x1, blocking collectives, shards(): bias_gradient = lax.psum(bias_local, ('dp', 'ctx'))  66.5 us
    reduce_scatter x1, waiting for transfers between devices, shards(): lax.psum_scatter(jnp.concatenate((key_block.reshape(row_total, feature_wi...  34 us
  transfers between devices with their start and end apart: 6, of which 5 were waited for; matrix products, arithmetic and copies ran while one was open for 6% of the time, Pallas kernels for 0%

commit v1 on v0

v1 whole, which is shorter than its diff:
```python
import jax
import jax.numpy as jnp
from jax import lax
from jax.sharding import PartitionSpec as P

H = 8
DH = 128
NB = 12
N_CTX = 4
EPSILON = 1e-05


def layer_norm(values):
    row_mean = jnp.mean(values, axis=-1, keepdims=True)
    centered = values - row_mean
    inverse = lax.rsqrt(jnp.mean(centered * centered, axis=-1, keepdims=True) + EPSILON)
    return (centered * inverse, inverse)


def norm_backward(unit_rows, inverse_rows, upstream_rows):
    mean_plain = jnp.mean(upstream_rows, axis=-1, keepdims=True)
    mean_cross = jnp.mean(upstream_rows * unit_rows, axis=-1, keepdims=True)
    return inverse_rows * (upstream_rows - mean_plain - unit_rows * mean_cross)


def silu_slope(values):
    logistic = jax.nn.sigmoid(values)
    return logistic * (1.0 + values * (1.0 - logistic))


def dot(a, b, dims):
    return lax.dot_general(a, b, (dims, ((), ())), preferred_element_type=jnp.float32)


def shards(tokens, send_rows, user_lengths, input_weight, output_weight, distance_bias, upstream):
    rows, width = tokens.shape
    groups = lax.axis_size("dp")
    slots = rows // groups
    length = rows * N_CTX
    cols = width // N_CTX
    scale = DH ** (-0.5)
    ctx = lax.axis_index("ctx")
    send_order = send_rows[0]
    lengths = user_lengths[0]
    ordered = jnp.take(tokens, send_order, axis=0).reshape(groups, slots, width)
    balanced = lax.all_to_all(ordered, "dp", split_axis=0, concat_axis=0, tiled=True).reshape(rows, width)
    features = balanced.astype(jnp.float32)
    unit_in, inverse_in = layer_norm(features)
    normed = lax.all_gather(unit_in.astype(jnp.bfloat16), "ctx", axis=0, tiled=True)
    own_weight = lax.dynamic_slice_in_dim(input_weight.reshape(width, 4, N_CTX, cols), ctx, 1, axis=2)
    own_weight = own_weight.reshape(width, 4 * cols)
    gg = dot(upstream, output_weight, ((1,), (1,))).astype(jnp.bfloat16)
    gg = lax.all_to_all(gg, "ctx", split_axis=1, concat_axis=0, tiled=True).astype(jnp.float32)

    projected = dot(normed, own_weight, ((1,), (0,)))
    activated = jax.nn.silu(projected).astype(jnp.bfloat16)
    gate, value, query, key = (activated[:, i * cols : (i + 1) * cols] for i in range(4))
    gate = gate.astype(jnp.float32)
    ends = jnp.cumsum(lengths)
    pos = jnp.arange(length)
    user = jnp.sum((pos[:, None] >= ends[None, :]).astype(jnp.int32), axis=1)
    dist = pos[:, None] - pos[None, :]
    visible = jnp.logical_and(user[:, None] == user[None, :], dist >= 0).astype(jnp.float32)
    bucket = jnp.zeros(dist.shape, jnp.int32)
    for level in range(1, NB):
        bucket = bucket + (dist + 1 >= 2**level).astype(jnp.int32)
    own_bias = lax.dynamic_slice_in_dim(distance_bias, ctx * 2, 2, axis=0)
    heads = []
    for h in range(2):
        s = slice(h * DH, (h + 1) * DH)
        bias = jnp.zeros(dist.shape, jnp.float32)
        for level in range(NB):
            bias = jnp.where(bucket == level, own_bias[h, level], bias)
        scores = dot(query[:, s], key[:, s], ((1,), (1,))) * scale + bias
        weights = (jax.nn.silu(scores) * visible).astype(jnp.bfloat16)
        att = dot(weights, value[:, s], ((1,), (0,)))
        heads.append((s, scores, weights, att))
    attended = jnp.concatenate([h[3] for h in heads], axis=1)
    g = gg * gate
    m = jnp.mean(attended, axis=1)
    cent = attended - m[:, None]
    stats = jnp.stack([m, jnp.sum(cent * cent, axis=1), jnp.sum(g, axis=1), jnp.sum(g * cent, axis=1)])
    alls = lax.all_gather(stats, "ctx", axis=0)
    mean = jnp.mean(alls[:, 0], axis=0)
    shift = alls[:, 0] - mean[None]
    var = (jnp.sum(alls[:, 1], axis=0) + cols * jnp.sum(shift * shift, axis=0)) / width
    inv = lax.rsqrt(var + EPSILON)
    g_mean = jnp.sum(alls[:, 2], axis=0) / width
    g_cross = inv * jnp.sum(alls[:, 3] + shift * alls[:, 2], axis=0) / width
    unit_out = (attended - mean[:, None]) * inv[:, None]
    gated = (unit_out * gate).astype(jnp.bfloat16)
    gated_own = lax.all_to_all(gated, "ctx", split_axis=0, concat_axis=1, tiled=True)
    layer_output = (features + dot(gated_own, output_weight, ((1,), (0,)))).astype(jnp.bfloat16)
    output_local = dot(gated_own, upstream, ((0,), (0,)))
    gate_gradient = gg * unit_out
    att_grad = (inv[:, None] * (g - g_mean[:, None] - unit_out * g_cross[:, None])).astype(jnp.bfloat16)
    dq, dk, dv, db = [], [], [], []
    for s, scores, weights, _ in heads:
        dw = dot(att_grad[:, s], value[:, s], ((1,), (1,)))
        ds = dw * silu_slope(scores) * visible
        db.append(jnp.stack([jnp.sum(jnp.where(bucket == level, ds, 0.0)) for level in range(NB)]))
        dsr = ds.astype(jnp.bfloat16)
        dq.append(dot(dsr, key[:, s], ((1,), (0,))) * scale)
        dk.append(dot(dsr, query[:, s], ((0,), (0,))) * scale)
        dv.append(dot(weights, att_grad[:, s], ((0,), (0,))))
    joined = jnp.concatenate([gate_gradient] + dv + dq + dk, axis=1)
    pg = (joined * silu_slope(projected)).astype(jnp.bfloat16)
    gin = dot(normed, pg, ((0,), (0,))).astype(jnp.bfloat16)
    ng = dot(pg, own_weight, ((1,), (1,))).astype(jnp.bfloat16)
    ng = lax.all_to_all(ng.reshape(N_CTX, rows, width), "ctx", split_axis=0, concat_axis=0, tiled=True)
    ng = jnp.sum(ng.astype(jnp.float32), axis=0)
    balanced_gradient = (upstream.astype(jnp.float32) + norm_backward(unit_in, inverse_in, ng)).astype(jnp.bfloat16)
    returned = lax.all_to_all(
        balanced_gradient.reshape(groups, slots, width), "dp", split_axis=0, concat_axis=0, tiled=True
    )
    token_gradient = jnp.zeros_like(tokens).at[send_order].set(returned.reshape(rows, width))
    per = width // groups
    gin = lax.all_to_all(gin.reshape(groups, per, width), "dp", split_axis=0, concat_axis=0, tiled=True)
    gin = jnp.sum(gin.astype(jnp.float32), axis=0)
    gin = lax.all_to_all(gin.reshape(N_CTX, per // N_CTX, width), "ctx", split_axis=0, concat_axis=0, tiled=True)
    gin = gin.reshape(N_CTX, per // N_CTX, 4, cols).transpose(1, 2, 0, 3).reshape(per // N_CTX, 4 * width)
    gout = output_local.astype(jnp.bfloat16)
    gout = lax.all_to_all(gout.reshape(groups, per, width), "dp", split_axis=0, concat_axis=0, tiled=True)
    gout = jnp.sum(gout.astype(jnp.float32), axis=0)
    gout = lax.psum_scatter(gout, "ctx", scatter_dimension=0, tiled=True)
    own_db = lax.dynamic_update_slice_in_dim(jnp.zeros((H, NB), jnp.float32), jnp.stack(db), ctx * 2, axis=0)
    own_db = jnp.pad(own_db, ((0, 0), (0, 128 - NB)))
    by_ctx = jnp.sum(lax.all_gather(own_db, "ctx", axis=0), axis=0)
    bias_gradient = jnp.sum(lax.all_gather(by_ctx, "dp", axis=0), axis=0)[:, :NB]
    return (layer_output, token_gradient, gin, gout, bias_gradient)


def solution(mesh):
    block = P(("dp", "ctx"), None)
    in_specs = (block, block, P("dp", None), P(), P(), P(), block)
    out_specs = (block, block, block, block, P())
    return jax.shard_map(shards, mesh=mesh, in_specs=in_specs, out_specs=out_specs, check_vma=False)
```

time: 1520 us -> 350 us (0.23)
  waiting for transfers between devices: 1250 us -> 65.2 us
  starting transfers between devices: 7.94 us -> 32.3 us
  blocking collectives: 84.9 us -> 67.1 us
  local copies, waits for them, and re-layouts: 35.7 us -> 52.2 us
    reduce_scatter x3 -> x1, waiting for transfers between devices: 1220 us -> 4.57 us  [shards(): gout = lax.psum_scatter(gout, 'ctx', scatter_dimension=0, tiled=True)]
    psum x1 -> x0, blocking collectives: 66.5 us -> none  [shards(): bias_gradient = lax.psum(bias_local, ('dp', 'ctx'))]
    all_to_all x1 -> x7, waiting for transfers between devices: 0.01 us -> 50.8 us  [the longest x1 25.8 us: shards(): lax.all_to_all(gin.reshape(groups, per, width), 'dp', split_axis=0, conca...]
    all_gather x0 -> x3, blocking collectives: none -> 48.7 us  [the longest x1 24.8 us: shards(): lax.all_gather(by_ctx, 'dp', axis=0)]
    all_to_all x1 -> x7, starting transfers between devices: 7.44 us -> 32.2 us  [the longest x1 5.77 us: shards(): lax.all_to_all(gg, 'ctx', split_axis=1, concat_axis=0, tiled=True)]
    all_gather x2 -> x1, waiting for transfers between devices: 26.9 us -> 9.77 us  [shards(): lax.all_gather(unit_in.astype(jnp.bfloat16), 'ctx', axis=0, tiled=True)]
    dot_general x14 -> x18, matrix products: 97.4 us -> 88.1 us  [dot(): lax.dot_general(a, b, (dims, ((), ())), preferred_element_type=jnp.float32)]
  transfers between devices with their start and end apart: 6 -> 9, of which waited for: 5 -> 6; matrix products, arithmetic and copies ran while one was open for 6% -> 33% of each run, Pallas kernels for 0% -> 0%
where the time goes in v1:
time: 350 us; the launch traced here: 346 us
  matrix products  88.1 us (25%)
  blocking collectives  67.1 us (19%)
  waiting for transfers between devices  65.2 us (19%)
  local copies, waits for them, and re-layouts  52.2 us (15%)
  starting transfers between devices  32.3 us (9%)
  other arithmetic  26 us (7%)
  between operations  14.6 us (4%)
    dot_general x18, matrix products, dot(): lax.dot_general(a, b, (dims, ((), ())), preferred_element_type=jnp.float32)  88.1 us
    all_to_all x1, waiting for transfers between devices, shards(): lax.all_to_all(gin.reshape(groups, per, width), 'dp', split_axis=0, conca...  25.8 us
    all_gather x1, blocking collectives, shards(): lax.all_gather(by_ctx, 'dp', axis=0)  24.8 us
    unnamed x37, local copies, waits for them, and re-layouts  19 us
    all_to_all x1, blocking collectives, shards(): lax.all_to_all(ordered, 'dp', split_axis=0, concat_axis=0, tiled=True)  18.4 us
    all_to_all x1, waiting for transfers between devices, shards(): lax.all_to_all(ng.reshape(N_CTX, rows, width), 'ctx', split_axis=0, conca...  17.8 us
    another operation x2, local copies, waits for them, and re-layouts, shards(): jnp.stack([jnp.sum(jnp.where(bucket == level, ds, 0.0)) for level in rang...  15.1 us
    all_gather x1, blocking collectives, shards(): alls = lax.all_gather(stats, 'ctx', axis=0)  12 us
  transfers between devices with their start and end apart: 9, of which 6 were waited for; matrix products, arithmetic and copies ran while one was open for 33% of the time, Pallas kernels for 0%

profile of v1, /device:TPU:0, one launch (start us, length us, event | category | flops | bytes accessed | tf_op | source)
XLA Modules:
  0.0 345.6 jit_solution(17533645958206098069)
XLA Ops:
  7.2 0.8 compare_select_fusion.1
  8.6 1.3 reduce.12
  10.0 2.7 gather_fusion
  12.9 18.4 %all_to_all.62 = bf16[32,8,1024]{2,1,0:T(8,128)(2,1)S(1)} all-to-all(bf16[32,8,1024]{2,1,0:T(8,128)(2,1)S(1)} %bitcast_select_fusion), channel_id=1, replica_groups=mesh['dp'=32,'ctx'=4] {'dp'}, dimensions={0} | all-to-all | bytes 1048576 | tf_op jit(solution)/shard_map/all_to_all | solution.py:46
  31.9 1.1 fusion.29
  33.0 0.7 convolution_convert_fusion.3
  33.8 0.8 copy.102
  34.6 5.8 %all-to-all-start.1 = ((bf16[256,4,256]{2,0,1:T(8,128)(2,1)}), bf16[256,4,256]{2,0,1:T(8,128)(2,1)S(1)}, u32[]{:S(2)}, u32[]{:S(2)}) async-start(bf16[256,4,256]{2,0,1:T(8,128)(2,1)} %bitcast.171), calls=%async_computation.1 | async-start | bytes 1048576 | tf_op jit(solution)/shard_map/all_to_all | solution.py:53
  40.4 12.0 %copy.63 = bf16[1024,4096]{0,1:T(8,128)(2,1)} copy(bf16[1024,4096]{1,0:T(8,128)(2,1)} %param.10) | data formatting | bytes 16777216 | tf_op args[3]
  52.6 0.7 constant_dynamic-slice_fusion
  53.3 0.7 fusion.65
  54.0 0.7 fusion.64
  54.8 3.1 constant_dynamic-slice_fusion.1
  57.9 9.8 %all-gather.6.cloned.1.call-done = bf16[1024,1024]{1,0:T(8,128)(2,1)} async-done(((bf16[256,1024]{1,0:T(8,128)(2,1)}), bf16[1024,1024]{1,0:T(8,128)(2,1)}) %all-gather.6.cloned.1.call-update) | async-done | bytes 2097168 | tf_op jit(solution)/shard_map/all_gather | solution.py:49
  67.7 6.9 %multiply_convert_fusion.1 = (bf16[1024,1024]{1,0:T(8,128)(2,1)S(1)}, f32[1024,1024]{1,0:T(8,128)}) fusion(bf16[1024,1024]{1,0:T(8,128)(2,1)} %all-gather.6.cloned.1.call-done, bf16[1024,1024]{0,1:T(8,128)(2,1)} %bitcast.167), kind=kOutput, calls=%fused_computation.40 | convolution fusion | flops 2152726528 | bytes 10485760 | tf_op jit(solution)/shard_map/dot_general | solution.py:32
  74.5 9.8 %select_add_fusion.1 = f32[1024,1024]{1,0:T(8,128)S(1)} fusion(f32[]{:T(128)} %bitcast.19, f32[]{:T(128)} %bitcast.18, f32[]{:T(128)} %bitcast.17, f32[]{:T(128)} %bitcast.16, f32[]{:T(128)} %bitcast.15, f32[]{:T(128)} %bitcast.14, f32[]{:T(128)} %bitcast.13, f32[]{:T(128)} %bitcast.12, f32[]{:T(128)} %bitcast.11, f32[]{:T(128)} %bitcast.10, f32[]{:T(128)} %bitcast.9, ...), kind=kOutput, calls=%fused_computation.38 | convolution fusion | flops 331350016 | bytes 4718640 | tf_op jit(solution)/shard_map/dot_general | solution.py:32
  84.4 19.7 %select_convert_fusion = (bf16[1024,1024]{1,0:T(8,128)(2,1)S(1)}, bf16[1024,1024]{1,0:T(8,128)(2,1)}, f32[1024,1024]{1,0:T(8,128)}) fusion(s32[1024]{0:T(1024)S(1)} %convert_reduce_fusion.5, f32[1024,1024]{1,0:T(8,128)S(1)} %select_add_fusion.1, f32[]{:T(128)} %bitcast.31, f32[]{:T(128)} %bitcast.30, f32[]{:T(128)} %bitcast.29, f32[]{:T(128)} %bitcast.28, ...), kind=kOutput, calls=%fused_computation.33 | convolution fusion | flops 347078656 | bytes 13115440 | tf_op jit(solution)/shard_map/dot_general | solution.py:32
  104.1 1.3 copy-done.1
  105.4 1.6 fusion.67
  107.0 2.1 copy.65
  109.1 3.2 fusion.66
  112.3 2.1 copy.64
  114.4 2.3 fusion.38
  116.7 12.0 %all-gather.3 = f32[4,4,1024]{2,1,0:T(4,128)S(1)} all-gather(f32[1,4,1024]{2,1,0:T(4,128)S(1)} %maximum_bitcast_fusion), channel_id=2, replica_groups=mesh['dp'=32,'ctx'=4] {'ctx'}, dimensions={0}, use_global_device_ids=true | all-gather | bytes 81920 | tf_op jit(solution)/shard_map/all_gather | solution.py:83
  128.8 2.9 multiply_convert_fusion.2
  131.7 13.7 %select_reduce_fusion.12 = (f32[]{:T(128)}, f32[]{:T(128)}, f32[]{:T(128)}, f32[]{:T(128)}, f32[]{:T(128)}, /*index=5*/f32[]{:T(128)}, f32[]{:T(128)}, f32[]{:T(...) fusion(f32[1024,1024]{1,0:T(8,128)S(1)} %copy-done.15, ...), kind=kOutput, calls=%fused_computation.16 | convolution fusion | flops 355467264 | bytes 6823984 | tf_op jit(solution)/shard_map/dot_general | solution.py:32
  145.5 13.7 %select_reduce_fusion = (f32[]{:T(128)}, f32[]{:T(128)}, f32[]{:T(128)}, f32[]{:T(128)}, f32[]{:T(128)}, /*index=5*/f32[]{:T(128)}, f32[]{:T(128)}, f32[]{:T(128...) fusion(f32[1024,1024]{1,0:T(8,128)S(1)} %copy-done.16, ...), kind=kOutput, calls=%fused_computation.4 | convolution fusion | flops 355467264 | bytes 6823984 | tf_op jit(solution)/shard_map/dot_general | solution.py:32
  159.4 0.8 convolution_dynamic-update-slice_fusion.1
  160.1 0.7 copy-done.2
  160.8 0.8 convolution_dynamic-update-slice_fusion
  161.6 0.7 fusion.22
  162.3 0.7 fusion.21
  163.0 0.8 fusion.20
  163.8 0.8 fusion.19
  164.5 2.0 copy-done.5
  166.5 1.0 copy.68
  167.5 3.7 %all-to-all-start.2 = ((bf16[4,256,256]{1,2,0:T(8,128)(2,1)}), bf16[4,256,256]{1,2,0:T(8,128)(2,1)S(1)}, u32[]{:S(2)}, u32[]{:S(2)}) async-start(bf16[4,256,256]{1,2,0:T(8,128)(2,1)} %copy.68), calls=%async_computation.2 | async-start | bytes 1048576 | tf_op jit(solution)/shard_map/all_to_all | solution.py:92
  171.2 5.0 %multiply_convert_fusion = bf16[1024,1024]{1,0:T(8,128)(2,1)S(1)} fusion(f32[1024,1024]{1,0:T(8,128)} %copy-done.5, f32[1024,1024]{1,0:T(8,128)} %get-tuple-element.74), kind=kLoop, calls=%fused_computation.30 | loop fusion | flops 9437184 | bytes 10485760 | tf_op jit(solution)/shard_map/convert_element_type | solution.py:107
  176.3 1.3 copy-done.8
  177.6 3.7 %convolution_convert_fusion.2 = bf16[1024,1024]{1,0:T(8,128)(2,1)} fusion(bf16[1024,1024]{1,0:T(8,128)(2,1)S(1)} %multiply_convert_fusion, bf16[1024,1024]{0,1:T(8,128)(2,1)S(1)} %bitcast.168), kind=kOutput, calls=%fused_computation.71 | convolution fusion | flops 2148532224 | bytes 6291456 | tf_op jit(solution)/shard_map/dot_general | solution.py:32
  181.3 4.8 %all-to-all-start.3 = ((bf16[4,256,1024]{2,1,0:T(8,128)(2,1)}), bf16[4,256,1024]{2,1,0:T(8,128)(2,1)}, u32[]{:S(2)}, u32[]{:S(2)}) async-start(bf16[4,256,1024]{2,1,0:T(8,128)(2,1)} %bitcast.169), calls=%async_computation.3 | async-start | bytes 4194304 | tf_op jit(solution)/shard_map/all_to_all | solution.py:110
  186.0 5.9 %convolution_convert_fusion.1 = bf16[1024,1024]{1,0:T(8,128)(2,1)} fusion(bf16[1024,1024]{1,0:T(8,128)(2,1)} %all-gather.6.cloned.1.call-done, bf16[1024,1024]{1,0:T(8,128)(2,1)} %copy-done.8), kind=kOutput, calls=%fused_computation.70 | convolution fusion | flops 2148532224 | bytes 6291456 | tf_op jit(solution)/shard_map/dot_general | solution.py:32
  192.0 17.8 %all-to-all-done.3 = bf16[4,256,1024]{2,1,0:T(8,128)(2,1)} async-done(((bf16[4,256,1024]{2,1,0:T(8,128)(2,1)}), bf16[4,256,1024]{2,1,0:T(8,128)(2,1)}, u32[]{:S(2)}, u32[]{:S(2)}) %all-to-all-start.3) | async-done | bytes 2097184 | tf_op jit(solution)/shard_map/all_to_all | solution.py:110
  209.7 4.8 %all-to-all-start.5 = ((bf16[32,32,1024]{2,1,0:T(8,128)(2,1)}), bf16[32,32,1024]{2,1,0:T(8,128)(2,1)}, u32[]{:S(2)}, u32[]{:S(2)}) async-start(bf16[32,32,1024]{2,1,0:T(8,128)(2,1)} %bitcast.170), calls=%async_computation.5 | async-start | bytes 4194304 | tf_op jit(solution)/shard_map/all_to_all | solution.py:118
  214.5 3.1 convolution_convert_fusion
  217.6 25.8 %all-to-all-done.5 = bf16[32,32,1024]{2,1,0:T(8,128)(2,1)} async-done(((bf16[32,32,1024]{2,1,0:T(8,128)(2,1)}), bf16[32,32,1024]{2,1,0:T(8,128)(2,1)}, u32[]{:S(2)}, u32[]{:S(2)}) %all-to-all-start.5) | async-done | bytes 2097184 | tf_op jit(solution)/shard_map/all_to_all | solution.py:118
  243.4 4.8 %all-to-all-start.7 = ((bf16[32,32,1024]{2,1,0:T(8,128)(2,1)}), bf16[32,32,1024]{2,1,0:T(8,128)(2,1)}, u32[]{:S(2)}, u32[]{:S(2)}) async-start(bf16[32,32,1024]{2,1,0:T(8,128)(2,1)} %bitcast.164), calls=%async_computation.7 | async-start | bytes 4194304 | tf_op jit(solution)/shard_map/all_to_all | solution.py:123
  248.1 7.7 %stack.116 = f32[12]{0:T(128)S(1)} concatenate(f32[1]{0:T(128)} %bitcast.54, f32[1]{0:T(128)} %bitcast.55, f32[1]{0:T(128)} %bitcast.56, f32[1]{0:T(128)} %bitcast.57, f32[1]{0:T(128)} %bitcast.58, f32[1]{0:T(128)} %bitcast.59, f32[1]{0:T(128)} %bitcast.60, f32[1]{0:T(128)} %bitcast.61, f32[1]{0:T(128)} %bitcast.62, f32[1]{0:T(128)} %bitcast.63, f32[1]{0:T(128)} %bitcast.64, ...), dimensions={0} | concatenate | bytes 96 | tf_op jit(solution)/shard_map/stack | solution.py:101
  255.8 7.5 %stack.130 = f32[12]{0:T(128)S(1)} concatenate(f32[1]{0:T(128)} %bitcast.67, f32[1]{0:T(128)} %bitcast.68, f32[1]{0:T(128)} %bitcast.69, f32[1]{0:T(128)} %bitcast.70, f32[1]{0:T(128)} %bitcast.71, f32[1]{0:T(128)} %bitcast.72, f32[1]{0:T(128)} %bitcast.73, f32[1]{0:T(128)} %bitcast.74, f32[1]{0:T(128)} %bitcast.75, f32[1]{0:T(128)} %bitcast.76, f32[1]{0:T(128)} %bitcast.77, ...), dimensions={0} | concatenate | bytes 96 | tf_op jit(solution)/shard_map/stack | solution.py:101
  263.3 11.9 %all-gather.1 = f32[32,128]{1,0:T(8,128)S(1)} all-gather(f32[8,128]{1,0:T(8,128)S(1)} %pad.4), channel_id=3, replica_groups=mesh['dp'=32,'ctx'=4] {'ctx'}, dimensions={0}, use_global_device_ids=true | all-gather | bytes 20480 | tf_op jit(solution)/shard_map/all_gather | solution.py:128
  275.3 24.8 %all-gather.2 = f32[256,128]{1,0:T(8,128)S(1)} all-gather(f32[8,128]{1,0:T(8,128)S(1)} %bitcast_reduce_fusion.1), channel_id=4, replica_groups=mesh['dp'=32,'ctx'=4] {'dp'}, dimensions={0}, use_global_device_ids=true | all-gather | bytes 135168 | tf_op jit(solution)/shard_map/all_gather | solution.py:129
  300.1 2.8 convert_reduce_fusion
  302.9 1.0 copy-done.4
  304.3 2.6 fusion.39
  306.9 5.1 %all-to-all-start.4 = ((bf16[32,8,1024]{2,1,0:T(8,128)(2,1)}), bf16[32,8,1024]{2,1,0:T(8,128)(2,1)}, u32[]{:S(2)}, u32[]{:S(2)}) async-start(bf16[32,8,1024]{2,1,0:T(8,128)(2,1)} %fusion.39), calls=%async_computation.4 | async-start | bytes 1048576 | tf_op jit(solution)/shard_map/all_to_all | solution.py:113
  312.7 2.6 convert_reduce_fusion.3
  315.3 2.6 convert_reduce_fusion.2
  317.9 5.2 %all-to-all-done.4 = bf16[32,8,1024]{2,1,0:T(8,128)(2,1)} async-done(((bf16[32,8,1024]{2,1,0:T(8,128)(2,1)}), bf16[32,8,1024]{2,1,0:T(8,128)(2,1)}, u32[]{:S(2)}, u32[]{:S(2)}) %all-to-all-start.4) | async-done | bytes 524320 | tf_op jit(solution)/shard_map/all_to_all | solution.py:113
  323.1 3.3 all-to-all-start.6
  326.5 1.5 fusion.16
  328.0 2.9 scatter_custom_fusion
  330.9 2.1 all-to-all-done.6
  333.2 0.7 reshape.234
  333.9 4.6 %reduce-scatter.2.cloned.1.call-done = f32[8,1024]{1,0:T(8,128)} async-done(((f32[32,1024]{1,0:T(8,128)}), f32[8,1024]{1,0:T(8,128)}) %reduce-scatter.2.cloned.1.call-update) | async-done | bytes 32784 | tf_op jit(solution)/shard_map/reduce_scatter | solution.py:125
  (67 shorter events, 3.3 us)
Async XLA Ops:
  7.2 25.8 %copy-start = (bf16[1024,1024]{1,0:T(8,128)(2,1)S(1)}, bf16[1024,1024]{1,0:T(8,128)(2,1)}, u32[]{:S(2)}) copy-start(bf16[1024,1024]{1,0:T(8,128)(2,1)} %param.11) | copy-start | bytes 6291460
  7.2 60.5 %all-gather.6.cloned.1.call-start = ((), (), s32[]{:S(2)}) async-start(), calls=%async_computation.9 | async-start | bytes 2621440 | tf_op jit(solution)/shard_map/all_gather | solution.py:49
  8.0 0.5 copy-start.12
  10.0 23.0 %copy-start.10 = (bf16[256,1024]{1,0:T(8,128)(2,1)S(1)}, bf16[256,1024]{1,0:T(8,128)(2,1)}, u32[]{:S(2)}) copy-start(bf16[256,1024]{1,0:T(8,128)(2,1)} %param.13) | copy-start | bytes 1572868
  34.6 79.8 %all-to-all-start.1 = ((bf16[256,4,256]{2,0,1:T(8,128)(2,1)}), bf16[256,4,256]{2,0,1:T(8,128)(2,1)S(1)}, u32[]{:S(2)}, u32[]{:S(2)}) async-start(bf16[256,4,256]{2,0,1:T(8,128)(2,1)} %bitcast.171), calls=%async_computation.1 | async-start | bytes 1048576 | tf_op jit(solution)/shard_map/all_to_all | solution.py:53
  40.4 12.1 %copy-start.13 = (s32[1,3]{1,0:T(1,128)S(1)}, s32[1,3]{1,0:T(1,128)}, u32[]{:S(2)}) copy-start(s32[1,3]{1,0:T(1,128)} %param.9) | copy-start | bytes 40
  74.5 29.5 %copy-start.6 = (bf16[1024,1024]{1,0:T(8,128)(2,1)}, bf16[1024,1024]{1,0:T(8,128)(2,1)S(1)}, u32[]{:S(2)}) copy-start(bf16[1024,1024]{1,0:T(8,128)(2,1)S(1)} %get-tuple-element.73) | copy-start | bytes 6291460
  84.4 19.7 %copy-start.14 = (f32[1024,1024]{1,0:T(8,128)}, f32[1024,1024]{1,0:T(8,128)S(1)}, u32[]{:S(2)}) copy-start(f32[1024,1024]{1,0:T(8,128)S(1)} %select_add_fusion.1) | copy-start | bytes 12582916
  104.0 1.3 copy-start.1
  114.4 17.4 %copy-start.7 = (bf16[1024,1024]{1,0:T(8,128)(2,1)S(1)}, bf16[1024,1024]{1,0:T(8,128)(2,1)}, u32[]{:S(2)}) copy-start(bf16[1024,1024]{1,0:T(8,128)(2,1)} %copy-done.6) | copy-start | bytes 6291460
  114.4 17.4 %copy-start.15 = (f32[1024,1024]{1,0:T(8,128)S(1)}, f32[1024,1024]{1,0:T(8,128)}, u32[]{:S(2)}) copy-start(f32[1024,1024]{1,0:T(8,128)} %copy-done.14) | copy-start | bytes 12582916
  131.7 13.7 %copy-start.16 = (f32[1024,1024]{1,0:T(8,128)S(1)}, f32[1024,1024]{1,0:T(8,128)}, u32[]{:S(2)}) copy-start(f32[1024,1024]{1,0:T(8,128)} %get-tuple-element.75) | copy-start | bytes 12582916
  145.5 13.9 %copy-start.3 = (bf16[1024,1024]{1,0:T(8,128)(2,1)S(1)}, bf16[1024,1024]{1,0:T(8,128)(2,1)}, u32[]{:S(2)}) copy-start(bf16[1024,1024]{1,0:T(8,128)(2,1)} %get-tuple-element.48) | copy-start | bytes 6291460
  159.2 1.6 copy-start.2
  163.0 3.5 %copy-start.11 = (bf16[1024,256]{1,0:T(8,128)(2,1)S(1)}, bf16[1024,256]{1,0:T(8,128)(2,1)}, u32[]{:S(2)}) copy-start(bf16[1024,256]{1,0:T(8,128)(2,1)} %get-tuple-element.42) | copy-start | bytes 1572868
  164.5 2.0 copy-start.5
  167.5 13.7 %all-to-all-start.2 = ((bf16[4,256,256]{1,2,0:T(8,128)(2,1)}), bf16[4,256,256]{1,2,0:T(8,128)(2,1)S(1)}, u32[]{:S(2)}, u32[]{:S(2)}) async-start(bf16[4,256,256]{1,2,0:T(8,128)(2,1)} %copy.68), calls=%async_computation.2 | async-start | bytes 1048576 | tf_op jit(solution)/shard_map/all_to_all | solution.py:92
  171.2 6.4 %copy-start.9 = (bf16[1024,4,1,256]{0,3,2,1:T(8,128)(2,1)S(1)}, bf16[1024,4,1,256]{0,3,2,1:T(8,128)(2,1)}, u32[]{:S(2)}) copy-start(bf16[1024,4,1,256]{0,3,2,1:T(8,128)(2,1)} %constant_dynamic-slice_fusion.1) | copy-start | bytes 6291460
  176.3 1.3 copy-start.8
  181.3 28.5 %all-to-all-start.3 = ((bf16[4,256,1024]{2,1,0:T(8,128)(2,1)}), bf16[4,256,1024]{2,1,0:T(8,128)(2,1)}, u32[]{:S(2)}, u32[]{:S(2)}) async-start(bf16[4,256,1024]{2,1,0:T(8,128)(2,1)} %bitcast.169), calls=%async_computation.3 | async-start | bytes 4194304 | tf_op jit(solution)/shard_map/all_to_all | solution.py:110
  209.7 33.6 %all-to-all-start.5 = ((bf16[32,32,1024]{2,1,0:T(8,128)(2,1)}), bf16[32,32,1024]{2,1,0:T(8,128)(2,1)}, u32[]{:S(2)}, u32[]{:S(2)}) async-start(bf16[32,32,1024]{2,1,0:T(8,128)(2,1)} %bitcast.170), calls=%async_computation.5 | async-start | bytes 4194304 | tf_op jit(solution)/shard_map/all_to_all | solution.py:118
  243.4 63.5 %all-to-all-start.7 = ((bf16[32,32,1024]{2,1,0:T(8,128)(2,1)}), bf16[32,32,1024]{2,1,0:T(8,128)(2,1)}, u32[]{:S(2)}, u32[]{:S(2)}) async-start(bf16[32,32,1024]{2,1,0:T(8,128)(2,1)} %bitcast.164), calls=%async_computation.7 | async-start | bytes 4194304 | tf_op jit(solution)/shard_map/all_to_all | solution.py:123
  302.9 1.0 copy-start.4
  306.9 16.3 %all-to-all-start.4 = ((bf16[32,8,1024]{2,1,0:T(8,128)(2,1)}), bf16[32,8,1024]{2,1,0:T(8,128)(2,1)}, u32[]{:S(2)}, u32[]{:S(2)}) async-start(bf16[32,8,1024]{2,1,0:T(8,128)(2,1)} %fusion.39), calls=%async_computation.4 | async-start | bytes 1048576 | tf_op jit(solution)/shard_map/all_to_all | solution.py:113
  312.0 26.5 %reduce-scatter.2.cloned.1.call-start = ((), (), s32[]{:S(2)}) async-start(), calls=%async_computation.10 | async-start | bytes 163840 | tf_op jit(solution)/shard_map/reduce_scatter | solution.py:125
  323.1 9.9 %all-to-all-start.6 = ((f32[4,8,1024]{2,1,0:T(8,128)}), f32[4,8,1024]{2,1,0:T(8,128)S(1)}, u32[]{:S(2)}, u32[]{:S(2)}) async-start(f32[4,8,1024]{2,1,0:T(8,128)} %bitcast.50), calls=%async_computation.6 | async-start | bytes 262144 | tf_op jit(solution)/shard_map/all_to_all | solution.py:120
Sparse Core Ops, SparseCore 0:
  33.1 34.5 all-gather.5
  318.0 20.4 reduce-scatter.1

commit v2 on v1

v2 whole, which is shorter than its diff:
```python
import jax
import jax.numpy as jnp
from jax import lax
from jax.experimental import pallas as pl
from jax.experimental.pallas import tpu as pltpu
from jax.sharding import PartitionSpec as P

H = 8
DH = 128
NB = 12
N_CTX = 4
R = 256
D = 1024
LEN = 1024
COLS = 256
HEADS = 2
EPSILON = 1e-05
SCALE = DH ** (-0.5)
F32 = jnp.float32
BF16 = jnp.bfloat16
MESH = pl.DeviceIdType.MESH
NN = ((1,), (0,))
NT = ((1,), (1,))
TN = ((0,), (0,))


def dot(left, right, dims):
    return lax.dot_general(left, right, (dims, ((), ())), preferred_element_type=F32)


def at(start, size):
    return pl.ds(pl.multiple_of(start, size), size)


def logistic(values):
    return 0.5 * jnp.tanh(0.5 * values) + 0.5


def copy_to(src, dst, send_sem, recv_sem, dp, ctx):
    return pltpu.make_async_remote_copy(
        src_ref=src, dst_ref=dst, send_sem=send_sem, recv_sem=recv_sem, device_id=(dp, ctx), device_id_type=MESH
    )


def split_halves(rows):
    count = rows.shape[0] // 8
    left = rows[:, :512].reshape(count, 1, 8, 512)
    right = rows[:, 512:].reshape(count, 1, 8, 512)
    return jnp.concatenate((left, right), axis=1).reshape(count * 16, 512)


def join_halves(pairs):
    count = pairs.shape[0] // 16
    parts = pairs.reshape(count, 2, 8, 512)
    return jnp.concatenate((parts[:, 0].reshape(count * 8, 512), parts[:, 1].reshape(count * 8, 512)), axis=1)


def kernel(
    tokens, send_rows, lengths, weight_in, weight_out, bias_table, upstream,
    layer_output, token_gradient, input_gradient, output_gradient, bias_gradient,
    w_in, w_out, pick, message, balanced, unit, inverse_in, normed, gg_send, gg_all, slope, act, bias_tile,
    w_tile, s_tile, attended, stats_send, stats_all, rows_stat, gated, gated_all, att_grad, dq, dk, dv, bias_sum, pg,
    ng_far, ng_far_in, ng_near, ng_near_in, ng_own, back, back_in,
    g_core, g_core_in, g_own, g_chip, g_chip_in, g_row, g_row_in,
    b_core, b_core_in, b_chip_in, b_row, b_row_in,
    w_sem, a_send, a_recv, gg_ssem, gg_rsem, z_send, z_recv, f_send, f_recv, st_send, st_recv, gt_send, gt_recv,
    nf_send, nf_recv, nn_send, nn_recv, r_send, r_recv, gc_send, gc_recv, gk_send, gk_recv, gr_send, gr_recv,
    bc_send, bc_recv, bk_send, bk_recv, br_send, br_recv,
):
    me = lax.axis_index("dp")
    ctx = lax.axis_index("ctx")
    plane, inner = me // 8, me % 8
    chip, core = me // 2, me % 2
    partner = chip * 2 + (1 - core)
    right, left, far = (ctx + 1) % 4, (ctx + 3) % 4, (ctx + 2) % 4

    out_copy = pltpu.make_async_copy(weight_out, w_out, w_sem.at[4])
    out_copy.start()
    in_copies = []
    for part in range(4):
        columns = pl.ds(pl.multiple_of(part * D + ctx * COLS, COLS), COLS)
        in_copies.append(pltpu.make_async_copy(weight_in.at[:, columns], w_in.at[part], w_sem.at[part]))
        in_copies[-1].start()

    barrier = pltpu.get_barrier_semaphore()

    @pl.loop(1, 32)
    def _(step):
        pl.semaphore_signal(barrier, inc=1, device_id=((me + step) % 32, ctx), device_id_type=MESH)

    for step in range(1, 4):
        pl.semaphore_signal(barrier, inc=1, device_id=(me, (ctx + step) % 4), device_id_type=MESH)

    rows_of = lax.broadcasted_iota(jnp.int32, (R, R), 0)
    pick[...] = jnp.where(rows_of == send_rows[...], 1.0, 0.0).astype(BF16)
    message[...] = split_halves(dot(pick[...], tokens[...], TN)).astype(BF16)

    pl.semaphore_wait(barrier, 34)

    def token_copy(dst):
        return copy_to(
            message.at[at(dst * 16, 16), :], balanced.at[at(me * 16, 16), :], a_send.at[dst], a_recv.at[me], dst, ctx
        )

    def token_arrival(src):
        return copy_to(
            message.at[at(src * 16, 16), :], balanced.at[at(src * 16, 16), :], a_send.at[src], a_recv.at[src], src, ctx
        )

    @pl.loop(1, 32)
    def _(step):
        p, q = step // 8, step % 8
        token_copy((plane + p) % 4 * 8 + (inner + q) % 8).start()

    balanced[at(me * 16, 16), :] = message[at(me * 16, 16), :]

    out_copy.wait()

    def gg_copy(block):
        return copy_to(
            gg_send.at[block], gg_all.at[ctx], gg_ssem.at[block], gg_rsem.at[ctx], me, block
        )

    for step in (2, 1, 3, 0):
        block = (ctx + step) % 4
        result = dot(upstream[...], w_out[at(block * COLS, COLS), :], NT).astype(BF16)
        if step == 0:
            gg_all[ctx] = result
        else:
            gg_send[block] = result
            gg_copy(block).start()

    def near_copy(p, side):
        rows = at(ctx * R + (plane + 4 - p) % 4 * 64, 64)
        return copy_to(
            normed.at[rows, :], normed.at[rows, :], z_send.at[side, p], z_recv.at[side, p], me, right if side == 0 else left
        )

    def near_arrival(p, side):
        rows = at((left if side == 0 else right) * R + (plane + 4 - p) % 4 * 64, 64)
        return copy_to(
            normed.at[rows, :], normed.at[rows, :], z_send.at[side, p], z_recv.at[side, p], me, right if side == 0 else left
        )

    def far_copy(p, side):
        rows = at((left if side == 0 else right) * R + (plane + 4 - p) % 4 * 64, 64)
        return copy_to(
            normed.at[rows, :], normed.at[rows, :], f_send.at[p], f_recv.at[p], me, right if side == 0 else left
        )

    def far_arrival(p, side):
        rows = at(far * R + (plane + 4 - p) % 4 * 64, 64)
        return copy_to(
            normed.at[rows, :], normed.at[rows, :], f_send.at[p], f_recv.at[p], me, right if side == 0 else left
        )

    for p in range(4):
        source = (plane + 4 - p) % 4

        @pl.loop(1 if p == 0 else 0, 8)
        def _(q):
            token_arrival(source * 8 + (inner + 8 - q) % 8).wait_recv()

        rows = join_halves(balanced[at(source * 128, 128), :].astype(F32))
        mean = jnp.mean(rows, axis=1, keepdims=True)
        centered = rows - mean
        inverse = lax.rsqrt(jnp.mean(centered * centered, axis=1, keepdims=True) + EPSILON)
        values = centered * inverse
        unit[at(source * 64, 64), :] = values
        inverse_in[at(source * 64, 64), :] = jnp.broadcast_to(inverse, (64, 128))
        normed[at(ctx * R + source * 64, 64), :] = values.astype(BF16)
        near_copy(p, 0).start()
        near_copy(p, 1).start()

    for part in range(4):
        in_copies[part].wait()

    def project(block):
        @pl.loop(0, 4)
        def _(part):
            values = dot(normed[at(block * R, R), :], w_in[part], NN)
            gate = logistic(values)
            active = values * gate
            act[part, at(block * R, R), :] = active.astype(BF16)
            slope[part, at(block * R, R), :] = gate + active * (1.0 - gate)

    for p in range(2):
        near_arrival(p, 0).wait_recv()
        far_copy(p, 0).start()

    for hh in range(HEADS):
        for r in range(3):
            reach = (
                lax.broadcasted_iota(jnp.int32, (R, R), 0) - lax.broadcasted_iota(jnp.int32, (R, R), 1) + (r * R + 1)
            )
            low, high = ((0, 8), (1, 9), (8, 9))[r]
            tile = jnp.full((R, R), bias_table[ctx * HEADS + hh, low], F32)
            for level in range(low + 1, high + 1):
                tile = jnp.where(reach >= 2**level, bias_table[ctx * HEADS + hh, level], tile)
            bias_tile[hh * 3 + r] = tile

    project(ctx)
    for p in range(2, 4):
        near_arrival(p, 1).wait_recv()
        far_copy(p, 1).start()
    near_arrival(2, 0).wait_recv()
    near_arrival(3, 0).wait_recv()
    project(left)
    near_arrival(0, 1).wait_recv()
    near_arrival(1, 1).wait_recv()
    project(right)
    far_arrival(0, 0).wait_recv()
    far_arrival(1, 0).wait_recv()
    far_arrival(2, 1).wait_recv()
    far_arrival(3, 1).wait_recv()
    project(far)

    end_0 = lengths[0, 0]
    end_1 = end_0 + lengths[0, 1]
    bases = (0, 4, 7)

    def seen(block, r):
        q_pos = lax.broadcasted_iota(jnp.int32, (R, R), 0) + block * R
        k_pos = lax.broadcasted_iota(jnp.int32, (R, R), 1) + (block - r) * R
        q_user = jnp.where(q_pos >= end_0, 1, 0) + jnp.where(q_pos >= end_1, 1, 0)
        k_user = jnp.where(k_pos >= end_0, 1, 0) + jnp.where(k_pos >= end_1, 1, 0)
        same = q_user == k_user
        if r == 0:
            same = jnp.logical_and(same, q_pos >= k_pos)
        return same

    for r in range(3):
        @pl.loop(r, 4)
        def _(block):
            visible = seen(block, r)
            for hh in range(HEADS):
                cols = slice(hh * DH, hh * DH + DH)
                query = act[2, at(block * R, R), cols]
                keys = act[3, at((block - r) * R, R), cols]
                values = act[1, at((block - r) * R, R), cols]
                scores = dot(query, keys, NT) * SCALE + bias_tile[hh * 3 + r]
                gate = logistic(scores)
                active = scores * gate
                weights = jnp.where(visible, active, 0.0).astype(BF16)
                s_tile[hh, bases[r] + block - r] = jnp.where(visible, gate + active * (1.0 - gate), 0.0)
                w_tile[hh, bases[r] + block - r] = weights
                term = dot(weights, values, NN)
                if r == 0:
                    attended[at(block * R, R), cols] = term
                else:
                    attended[at(block * R, R), cols] += term

    for step in range(1, 4):
        block = (ctx + step) % 4
        copy_to(gg_send.at[block], gg_all.at[block], gg_ssem.at[block], gg_rsem.at[block], me, block).wait_recv()

    lane = lax.broadcasted_iota(jnp.int32, (R, 128), 1)

    @pl.loop(0, 4)
    def _(block):
        rows = attended[at(block * R, R), :]
        mean = jnp.mean(rows, axis=1, keepdims=True)
        centered = rows - mean
        flow = gg_all[block].astype(F32) * act[0, at(block * R, R), :].astype(F32)
        packed = jnp.where(lane == 0, mean, 0.0)
        packed = jnp.where(lane == 1, jnp.sum(centered * centered, axis=1, keepdims=True), packed)
        packed = jnp.where(lane == 2, jnp.sum(flow, axis=1, keepdims=True), packed)
        packed = jnp.where(lane == 3, jnp.sum(flow * centered, axis=1, keepdims=True), packed)
        stats_send[block] = packed.T[:8, :]

    def stats_copy(block):
        return copy_to(stats_send, stats_all.at[ctx], st_send.at[block], st_recv.at[ctx], me, block)

    for step in range(1, 4):
        stats_copy((ctx + step) % 4).start()
    stats_all[ctx] = stats_send[...]
    for step in range(1, 4):
        block = (ctx + step) % 4
        copy_to(stats_send, stats_all.at[block], st_send.at[block], st_recv.at[block], me, block).wait_recv()

    for block in range(4):
        parts = [stats_all[c, block] for c in range(4)]
        means = [x[0:1] for x in parts]
        mean = (means[0] + means[1] + means[2] + means[3]) * 0.25
        square = sum(parts[c][1:2] + COLS * (means[c] - mean) * (means[c] - mean) for c in range(4))
        flow = sum(parts[c][2:3] for c in range(4))
        cross = sum(parts[c][3:4] + (means[c] - mean) * parts[c][2:3] for c in range(4))
        inverse = lax.rsqrt(square * (1.0 / D) + EPSILON)
        table = jnp.concatenate(
            (mean, inverse, flow * (1.0 / D), cross * inverse * (1.0 / D), jnp.zeros((124, R), F32)), axis=0
        )
        rows_stat[pl.ds(block * R, R), :] = table.T

    def gated_copy(block):
        return copy_to(gated.at[block], gated_all.at[ctx], gt_send.at[block], gt_recv.at[ctx], me, block)

    @pl.loop(0, 4)
    def _(block):
        rows = at(block * R, R)
        table = rows_stat[rows, :]
        inverse = table[:, 1:2]
        out_unit = (attended[rows, :] - table[:, 0:1]) * inverse
        gate = act[0, rows, :].astype(F32)
        flow = gg_all[block].astype(F32)
        gated[block] = (out_unit * gate).astype(BF16)
        pg[0, rows, :] = (flow * out_unit * slope[0, rows, :]).astype(BF16)
        att_grad[rows, :] = (inverse * (flow * gate - table[:, 2:3] - out_unit * table[:, 3:4])).astype(BF16)

    for step in range(1, 4):
        gated_copy((ctx + step) % 4).start()
    gated_all[ctx] = gated[ctx]

    def core_copy(which, piece):
        return copy_to(
            g_core.at[which, piece], g_core_in.at[which, piece], gc_send.at[which, piece], gc_recv.at[which, piece],
            partner, ctx,
        )

    def chip_copy(which, other):
        return copy_to(
            g_chip.at[which, other], g_chip_in.at[which, chip], gk_send.at[which, other], gk_recv.at[which, chip],
            other * 2 + core, ctx,
        )

    def chip_arrival(which, other):
        return copy_to(
            g_chip.at[which, other], g_chip_in.at[which, other], gk_send.at[which, other], gk_recv.at[which, other],
            other * 2 + core, ctx,
        )

    def row_copy(which, block):
        return copy_to(
            g_row.at[which, at(block * 8, 8), :], g_row_in.at[which, ctx], gr_send.at[which, block],
            gr_recv.at[which, ctx], me, block,
        )

    def row_arrival(which, block):
        return copy_to(
            g_row.at[which, at(block * 8, 8), :], g_row_in.at[which, block], gr_send.at[which, block],
            gr_recv.at[which, block], me, block,
        )

    def keep_tile(which, piece, column, tile):
        halves = tile.reshape(4, 2, 32, COLS)
        first, second = halves[:, 0].reshape(128, COLS), halves[:, 1].reshape(128, COLS)
        cols = at(column * COLS, COLS)
        g_own[which, piece, :, cols] = jnp.where(core == 0, first, second).astype(BF16)
        g_core[which, piece, :, cols] = jnp.where(core == 0, second, first).astype(BF16)

    def sum_cores(which):
        for piece in range(4):
            core_copy(which, piece).wait_recv()
            both = g_own[which, piece].astype(F32) + g_core_in[which, piece].astype(F32)
            g_chip[which, pl.ds(piece * 4, 4)] = both.astype(BF16).reshape(4, 32, D)

        @pl.loop(1, 16)
        def _(step):
            chip_copy(which, (chip + step) % 16).start()

        g_chip_in[which, chip] = g_chip[which, chip]

    def sum_chips(which):
        @pl.loop(1, 16)
        def _(step):
            chip_arrival(which, (chip + step) % 16).wait_recv()

        for column in range(4):
            cols = slice(column * COLS, column * COLS + COLS)
            total = g_chip_in[which, 0, :, cols].astype(F32)
            for other in range(1, 16):
                total = total + g_chip_in[which, other, :, cols].astype(F32)
            g_row[which, :, cols] = total
        for step in range(1, 4):
            row_copy(which, (ctx + step) % 4).start()
        g_row_in[which, ctx] = g_row[which, at(ctx * 8, 8), :]

    def attention_back(r):
        @pl.loop(r, 4)
        def _(block):
            q_rows = at(block * R, R)
            k_rows = at((block - r) * R, R)
            for hh in range(HEADS):
                cols = slice(hh * DH, hh * DH + DH)
                incoming = att_grad[q_rows, cols]
                change = dot(incoming, act[1, k_rows, cols], NT) * s_tile[hh, bases[r] + block - r]
                if r == 0:
                    first = jnp.where(block == 0, 0.0, 1.0)
                    bias_sum[hh * 3 + r] = bias_sum[hh * 3 + r] * first + change
                else:
                    bias_sum[hh * 3 + r] += change
                rounded = change.astype(BF16)
                q_term = dot(rounded, act[3, k_rows, cols], NN)
                k_term = dot(rounded, act[2, q_rows, cols], TN)
                v_term = dot(w_tile[hh, bases[r] + block - r], incoming, TN)
                if r == 0:
                    dq[q_rows, cols] = q_term
                    dk[k_rows, cols] = k_term
                    dv[k_rows, cols] = v_term
                else:
                    dq[q_rows, cols] += q_term
                    dk[k_rows, cols] += k_term
                    dv[k_rows, cols] += v_term

    bias_sum[...] = jnp.zeros((6, R, R), F32)
    attention_back(0)

    for step in range(1, 4):
        block = (ctx + step) % 4
        copy_to(gated.at[block], gated_all.at[block], gt_send.at[block], gt_recv.at[block], me, block).wait_recv()

    for piece in range(4):
        left_rows = gated_all[piece].T

        @pl.loop(0, 4)
        def _(column):
            keep_tile(1, piece, column, dot(left_rows, upstream[:, at(column * COLS, COLS)], NN))

        core_copy(1, piece).start()

    attention_back(1)
    sum_cores(1)
    attention_back(2)

    @pl.loop(0, 4)
    def _(block):
        rows = at(block * R, R)
        pg[1, rows, :] = (dv[rows, :] * slope[1, rows, :]).astype(BF16)
        pg[2, rows, :] = (dq[rows, :] * SCALE * slope[2, rows, :]).astype(BF16)
        pg[3, rows, :] = (dk[rows, :] * SCALE * slope[3, rows, :]).astype(BF16)

    def block_terms(block, half):
        rows = at(block * R, R)
        total = dot(pg[0, rows, :], w_in[0, half * 512 : half * 512 + 512, :], NT)
        for part in range(1, 4):
            total = total + dot(pg[part, rows, :], w_in[part, half * 512 : half * 512 + 512, :], NT)
        return total

    def far_part(side):
        return copy_to(
            ng_far.at[side], ng_far_in.at[side], nf_send.at[side], nf_recv.at[side], me, right if side == 0 else left
        )

    def near_part(side, half):
        return copy_to(
            ng_near.at[side, half], ng_near_in.at[side, half], nn_send.at[side, half], nn_recv.at[side, half], me,
            right if side == 0 else left,
        )

    for side in range(2):
        ng_far[side] = block_terms(far, side).astype(BF16)
        far_part(side).start()
    for side in range(2):
        ng_near[side, 1 - side] = block_terms(right if side == 0 else left, 1 - side).astype(BF16)
        near_part(side, 1 - side).start()
    for side in range(2):
        terms = block_terms(right if side == 0 else left, side)
        far_part(side).wait_recv()
        ng_near[side, side] = (terms + ng_far_in[side].astype(F32)).astype(BF16)
        near_part(side, side).start()
    for half in range(2):
        ng_own[:, half * 512 : half * 512 + 512] = block_terms(ctx, half)

    for piece in range(4):
        left_rows = normed[:, piece * R : piece * R + R].T

        @pl.loop(0, 4)
        def _(part):
            keep_tile(0, piece, part, dot(left_rows, pg[part], NN))

        core_copy(0, piece).start()
    sum_cores(0)

    for half in range(2):
        cols = slice(half * 512, half * 512 + 512)
        total = dot(gated_all[0], w_out[0:COLS, cols], NN)
        for c in range(1, 4):
            total = total + dot(gated_all[c], w_out[c * COLS : c * COLS + COLS, cols], NN)
        pairs = balanced[...].astype(F32).reshape(32, 2, 8, 512)
        layer_output[:, cols] = (pairs[:, half].reshape(R, 512) + total).astype(BF16)

    sums = jnp.zeros((8, 128), F32)
    tile_row = lax.broadcasted_iota(jnp.int32, (8, 128), 0)
    tile_lane = lax.broadcasted_iota(jnp.int32, (8, 128), 1)
    for hh in range(HEADS):
        for r in range(3):
            reach = (
                lax.broadcasted_iota(jnp.int32, (R, R), 0) - lax.broadcasted_iota(jnp.int32, (R, R), 1) + (r * R + 1)
            )
            low, high = ((0, 8), (1, 9), (8, 9))[r]
            tile = bias_sum[hh * 3 + r]
            for level in range(low, high + 1):
                part = tile
                if level > low:
                    part = jnp.where(reach >= 2**level, part, 0.0)
                if level < high:
                    part = jnp.where(reach < 2 ** (level + 1), part, 0.0)
                total = jnp.sum(jnp.sum(part, axis=0, keepdims=True), axis=1, keepdims=True)
                place = jnp.logical_and(tile_row == ctx * HEADS + hh, tile_lane == level)
                sums = sums + jnp.where(place, total, 0.0)
    b_core[...] = sums
    bias_core = copy_to(b_core, b_core_in, bc_send, bc_recv, partner, ctx)
    bias_core.start()

    for side in range(2):
        for half in range(2):
            near_part(side, half).wait_recv()

    def back_copy(dst):
        return copy_to(
            back.at[at(dst * 16, 16), :], back_in.at[at(me * 16, 16), :], r_send.at[dst], r_recv.at[me], dst, ctx
        )

    def back_arrival(src):
        return copy_to(
            back.at[at(src * 16, 16), :], back_in.at[at(src * 16, 16), :], r_send.at[src], r_recv.at[src], src, ctx
        )

    for p in range(4):
        target = (plane + p) % 4
        rows = at(target * 64, 64)
        total = []
        for half in range(2):
            total.append(
                ng_own[rows, half * 512 : half * 512 + 512]
                + ng_near_in[0, half, rows, :].astype(F32)
                + ng_near_in[1, half, rows, :].astype(F32)
            )
        total = jnp.concatenate(total, axis=1)
        values = unit[rows, :]
        plain = jnp.mean(total, axis=1, keepdims=True)
        cross = jnp.mean(total * values, axis=1, keepdims=True)
        change = inverse_in[rows, 0:1] * (total - plain - values * cross)
        result = upstream[rows, :].astype(F32) + change
        back[at(target * 128, 128), :] = split_halves(result).astype(BF16)

        @pl.loop(1 if p == 0 else 0, 8)
        def _(q):
            back_copy(target * 8 + (inner + q) % 8).start()

    back_in[at(me * 16, 16), :] = back[at(me * 16, 16), :]

    bias_core.wait_recv()
    b_chip_in[chip] = b_core[...] + b_core_in[...]

    def bias_chip(other):
        return copy_to(
            b_chip_in.at[chip], b_chip_in.at[chip], bk_send.at[other], bk_recv.at[chip], other * 2 + core, ctx
        )

    @pl.loop(1, 16)
    def _(step):
        bias_chip((chip + step) % 16).start()

    sum_chips(1)
    sum_chips(0)

    @pl.loop(1, 16)
    def _(step):
        other = (chip + step) % 16
        copy_to(
            b_chip_in.at[other], b_chip_in.at[other], bk_send.at[other], bk_recv.at[other], other * 2 + core, ctx
        ).wait_recv()

    total = b_chip_in[0]
    for other in range(1, 16):
        total = total + b_chip_in[other]
    b_row[...] = total
    b_row_in[ctx] = total
    for step in range(1, 4):
        block = (ctx + step) % 4
        copy_to(b_row, b_row_in.at[ctx], br_send.at[block], br_recv.at[ctx], me, block).start()

    @pl.loop(1, 32)
    def _(step):
        back_arrival((me + step) % 32).wait_recv()

    returned = join_halves(back_in[...].astype(F32)).astype(BF16)
    token_gradient[...] = dot(pick[...], returned, NN).astype(BF16)

    for step in range(1, 4):
        block = (ctx + step) % 4
        row_arrival(0, block).wait_recv()
        row_arrival(1, block).wait_recv()
        copy_to(b_row, b_row_in.at[block], br_send.at[block], br_recv.at[block], me, block).wait_recv()
    for c in range(4):
        for part in range(4):
            input_gradient[:, part * D + c * COLS : part * D + c * COLS + COLS] = g_row_in[
                0, c, :, part * COLS : part * COLS + COLS
            ]
    output_gradient[...] = g_row_in[1, 0] + g_row_in[1, 1] + g_row_in[1, 2] + g_row_in[1, 3]
    bias_gradient[...] = b_row_in[0] + b_row_in[1] + b_row_in[2] + b_row_in[3]

    @pl.loop(1, 32)
    def _(step):
        other = (me + step) % 32
        token_copy(other).wait_send()
        back_copy(other).wait_send()

    for p in range(4):
        near_copy(p, 0).wait_send()
        near_copy(p, 1).wait_send()
        far_copy(p, 0 if p < 2 else 1).wait_send()
    for step in range(1, 4):
        block = (ctx + step) % 4
        gg_copy(block).wait_send()
        stats_copy(block).wait_send()
        gated_copy(block).wait_send()
        row_copy(0, block).wait_send()
        row_copy(1, block).wait_send()
        copy_to(b_row, b_row_in.at[ctx], br_send.at[block], br_recv.at[ctx], me, block).wait_send()
    for side in range(2):
        far_part(side).wait_send()
        near_part(side, 0).wait_send()
        near_part(side, 1).wait_send()
    for which in range(2):
        for piece in range(4):
            core_copy(which, piece).wait_send()

        @pl.loop(1, 16)
        def _(step):
            chip_copy(which, (chip + step) % 16).wait_send()

    bias_core.wait_send()

    @pl.loop(1, 16)
    def _(step):
        bias_chip((chip + step) % 16).wait_send()


def shards(tokens, send_rows, user_lengths, input_weight, output_weight, distance_bias, upstream):
    vmem = pl.BlockSpec(memory_space=pltpu.VMEM)
    smem = pl.BlockSpec(memory_space=pltpu.SMEM)
    hbm = pl.BlockSpec(memory_space=pl.ANY)
    dma = pltpu.SemaphoreType.DMA
    V = pltpu.VMEM
    scratch = [
        V((4, D, COLS), BF16), V((D, D), BF16), V((R, R), BF16), V((512, 512), BF16), V((512, 512), BF16),
        V((R, D), F32), V((R, 128), F32), V((LEN, D), BF16), V((4, R, COLS), BF16), V((4, R, COLS), BF16),
        V((4, LEN, COLS), F32), V((4, LEN, COLS), BF16), V((6, R, R), F32),
        V((HEADS, 9, R, R), BF16), V((HEADS, 9, R, R), F32), V((LEN, COLS), F32),
        V((4, 8, R), F32), V((4, 4, 8, R), F32), V((LEN, 128), F32),
        V((4, R, COLS), BF16), V((4, R, COLS), BF16), V((LEN, COLS), BF16),
        V((LEN, COLS), F32), V((LEN, COLS), F32), V((LEN, COLS), F32), V((6, R, R), F32), V((4, LEN, COLS), BF16),
        V((2, R, 512), BF16), V((2, R, 512), BF16), V((2, 2, R, 512), BF16), V((2, 2, R, 512), BF16), V((R, D), F32),
        V((512, 512), BF16), V((512, 512), BF16),
        V((2, 4, 128, D), BF16), V((2, 4, 128, D), BF16), V((2, 4, 128, D), BF16),
        V((2, 16, 32, D), BF16), V((2, 16, 32, D), BF16), V((2, 32, D), F32), V((2, 4, 8, D), F32),
        V((8, 128), F32), V((8, 128), F32), V((16, 8, 128), F32), V((8, 128), F32), V((4, 8, 128), F32),
        dma((5,)), dma((32,)), dma((32,)), dma((4,)), dma((4,)), dma((2, 4)), dma((2, 4)), dma((4,)), dma((4,)),
        dma((4,)), dma((4,)), dma((4,)), dma((4,)),
        dma((2,)), dma((2,)), dma((2, 2)), dma((2, 2)), dma((32,)), dma((32,)),
        dma((2, 4)), dma((2, 4)), dma((2, 16)), dma((2, 16)), dma((2, 4)), dma((2, 4)),
        dma(()), dma(()), dma((16,)), dma((16,)), dma((4,)), dma((4,)),
    ]
    outs = pl.pallas_call(
        kernel,
        out_shape=(
            jax.ShapeDtypeStruct((R, D), BF16),
            jax.ShapeDtypeStruct((R, D), BF16),
            jax.ShapeDtypeStruct((8, 4 * D), F32),
            jax.ShapeDtypeStruct((8, D), F32),
            jax.ShapeDtypeStruct((8, 128), F32),
        ),
        in_specs=[vmem, vmem, smem, hbm, hbm, smem, vmem],
        out_specs=(vmem,) * 5,
        scratch_shapes=scratch,
        compiler_params=pltpu.CompilerParams(
            collective_id=0, has_side_effects=True, vmem_limit_bytes=60 * 1024 * 1024
        ),
        name="hstu_layer",
    )(tokens, send_rows, user_lengths, input_weight, output_weight, distance_bias, upstream)
    return outs[0], outs[1], outs[2], outs[3], outs[4][:, :NB]


def solution(mesh):
    block = P(("dp", "ctx"), None)
    in_specs = (block, block, P("dp", None), P(), P(), P(), block)
    out_specs = (block, block, block, block, P())
    return jax.shard_map(shards, mesh=mesh, in_specs=in_specs, out_specs=out_specs, check_vma=False)
```

time: 350 us -> 124 us (0.35)
  the two profiles are of different devices: /device:TPU:0 before, /device:TPU:4 now
where the time goes in v2:
time: 124 us; the launch traced here: 123 us
  Pallas kernels  115 us (93%)
  local copies, waits for them, and re-layouts  7.95 us (6%)
    pallas_call x1, Pallas kernels, shards(): pl.pallas_call(kernel, out_shape=(jax.ShapeDtypeStruct((R, D), BF16), jax...  115 us
    unnamed x5, local copies, waits for them, and re-layouts  7.95 us

profile of v2, /device:TPU:4, one launch (start us, length us, event | category | flops | bytes accessed | tf_op | source)
XLA Modules:
  0.0 123.3 jit_solution(8950769752137118908)
XLA Ops:
  0.6 114.7 %hstu_layer.1 = (bf16[256,1024]{1,0:T(8,128)(2,1)}, bf16[256,1024]{1,0:T(8,128)(2,1)}, f32[8,4096]{1,0:T(8,128)}, f32[8,1024]{1,0:T(8,128)}, f32[8,128]{1,0:T(8,128)}) custom-call(bf16[256,1024]{1,0:T(8,128)(2,1)} %tokens.1, s32[1,256]{1,0:T(1,128)} %send_rows.1, s32[1,3]{1,0:T(1,128)} %lengths.1, bf16[1024,4096]{1,0:T(8,128)(2,1)} %weight_in.1, ...), custom_call_target="tpu_custom_call" | custom-call | tf_op jit(solution)/shard_map/hstu_layer/pallas_call | solution.py:655
  115.3 1.9 %copy.17 = bf16[256,1024]{1,0:T(8,128)(2,1)} copy(bf16[256,1024]{1,0:T(8,128)(2,1)} %get-tuple-element.20) | data formatting | bytes 1048576
  117.2 1.9 %copy.18 = bf16[256,1024]{1,0:T(8,128)(2,1)} copy(bf16[256,1024]{1,0:T(8,128)(2,1)} %get-tuple-element.21) | data formatting | bytes 1048576
  119.0 1.6 %copy.19 = f32[8,4096]{1,0:T(8,128)} copy(f32[8,4096]{1,0:T(8,128)} %get-tuple-element.22) | data formatting | bytes 262144
  120.6 1.4 %copy.20 = f32[8,1024]{1,0:T(8,128)} copy(f32[8,1024]{1,0:T(8,128)} %get-tuple-element.23) | data formatting | bytes 65536
  122.0 1.3 %copy.21 = f32[8,12]{1,0:T(8,128)} copy(f32[8,12]{1,0:T(8,128)} %bitcast.1) | data formatting | bytes 768

commit v3 on v2

v3 whole, which is shorter than its diff:
```python
import jax
import jax.numpy as jnp
from jax import lax
from jax.experimental import pallas as pl
from jax.experimental.pallas import tpu as pltpu
from jax.sharding import PartitionSpec as P

PLANES = (0, 1, 3, 2)
AHEAD = 3

H = 8
DH = 128
NB = 12
N_CTX = 4
R = 256
D = 1024
LEN = 1024
COLS = 256
HEADS = 2
EPSILON = 1e-05
HIDDEN = -(2.0**40)
SCALE = DH ** (-0.5)
F32 = jnp.float32
BF16 = jnp.bfloat16
MESH = pl.DeviceIdType.MESH
NN = ((1,), (0,))
NT = ((1,), (1,))
TN = ((0,), (0,))


def dot(left, right, dims):
    return lax.dot_general(left, right, (dims, ((), ())), preferred_element_type=F32)


def at(start, size):
    return pl.ds(pl.multiple_of(start, size), size)


def silu_parts(halved):
    rise = 1.0 + jnp.tanh(halved)
    active = halved * rise
    return active, active + (0.5 * rise) * (1.0 - active)


def copy_to(src, dst, send_sem, recv_sem, dp, ctx):
    return pltpu.make_async_remote_copy(
        src_ref=src, dst_ref=dst, send_sem=send_sem, recv_sem=recv_sem, device_id=(dp, ctx), device_id_type=MESH
    )


def split_halves(rows):
    count = rows.shape[0] // 8
    left = rows[:, :512].reshape(count, 1, 8, 512)
    right = rows[:, 512:].reshape(count, 1, 8, 512)
    return jnp.concatenate((left, right), axis=1).reshape(count * 16, 512)


def join_halves(pairs):
    count = pairs.shape[0] // 16
    parts = pairs.reshape(count, 2, 8, 512)
    return jnp.concatenate((parts[:, 0].reshape(count * 8, 512), parts[:, 1].reshape(count * 8, 512)), axis=1)


def kernel(
    tokens, send_rows, lengths, weight_in, weight_out, bias_table, upstream,
    layer_output, token_gradient, input_gradient, output_gradient, bias_gradient,
    w_in, w_out, pick, message, balanced, unit, inverse_in, normed, gg_send, gg_all, slope, act, bias_tile,
    w_tile, s_tile, attended, stats_send, stats_all, rows_stat, gated, gated_all, att_grad, dq, dk, dv, bias_sum, pg, turned, q_user, k_user,
    ng_far, ng_far_in, ng_near, ng_near_in, ng_own, back, back_in,
    g_core, g_core_in, ga, ga_in, gb, gb_in, ha, ha_in, hb, hb_in, g_row, g_row_in,
    b_core, b_core_in, b_chip_in, b_row, b_row_in,
    w_sem, a_send, a_recv, gg_ssem, gg_rsem, z_send, z_recv, f_send, f_recv, st_send, st_recv, gt_send, gt_recv,
    nf_send, nf_recv, nn_send, nn_recv, r_send, r_recv, gc_send, gc_recv, ga_send, ga_recv, gb_send, gb_recv, ha_send, ha_recv, hb_send, hb_recv, gr_send, gr_recv,
    bc_send, bc_recv, bk_send, bk_recv, br_send, br_recv,
):
    me = lax.axis_index("dp")
    sent, due = [], {}
    def ring(n, base, fn):
        @pl.loop(1, n)
        def _(step):
            fn((base + step) % n)
    def take(key):
        due.pop(key)()
    ctx = lax.axis_index("ctx")
    plane, inner = me // 8, me % 8
    chip, core = me // 2, me % 2
    partner = chip * 2 + (1 - core)
    right, left, far = (ctx + 1) % 4, (ctx + 3) % 4, (ctx + 2) % 4
    x, y = chip // 4, chip % 4
    ordered = (ctx, right, left, far)

    out_copy = pltpu.make_async_copy(weight_out, w_out, w_sem.at[4])
    out_copy.start()
    in_copies = []
    for part in range(4):
        columns = pl.ds(pl.multiple_of(part * D + ctx * COLS, COLS), COLS)
        in_copies.append(pltpu.make_async_copy(weight_in.at[:, columns], w_in.at[:, pl.ds(part * COLS, COLS)], w_sem.at[part]))
        in_copies[-1].start()
    due["w4"] = out_copy.wait
    for part in range(4):
        due["w%d" % part] = in_copies[part].wait

    barrier = pltpu.get_barrier_semaphore()

    @pl.loop(1, 32)
    def _(step):
        pl.semaphore_signal(barrier, inc=1, device_id=((me + step) % 32, ctx), device_id_type=MESH)

    for step in range(1, 4):
        pl.semaphore_signal(barrier, inc=1, device_id=(me, (ctx + step) % 4), device_id_type=MESH)

    rows_of = lax.broadcasted_iota(jnp.int32, (R, R), 0)
    pick[...] = jnp.where(rows_of == send_rows[...], 1.0, 0.0).astype(BF16)
    message[...] = split_halves(dot(pick[...], tokens[...], TN)).astype(BF16)

    pl.semaphore_wait(barrier, 34)

    def token_copy(dst):
        return copy_to(
            message.at[at(dst * 16, 16), :], balanced.at[at(me * 16, 16), :], a_send.at[dst], a_recv.at[me], dst, ctx
        )

    def token_arrival(src):
        return copy_to(
            message.at[at(src * 16, 16), :], balanced.at[at(src * 16, 16), :], a_send.at[src], a_recv.at[src], src, ctx
        )

    def send_plane(p):
        @pl.loop(1 if p == 0 else 0, 8)
        def _(q):
            token_copy((plane + p) % 4 * 8 + (inner + q) % 8).start()

    for p in PLANES[:AHEAD]:
        send_plane(p)
    balanced[at(me * 16, 16), :] = message[at(me * 16, 16), :]
    sent.append(lambda: ring(32, me, lambda o: token_copy(o).wait_send()))

    take("w4")

    def gg_copy(block):
        return copy_to(
            gg_send.at[block], gg_all.at[ctx], gg_ssem.at[block], gg_rsem.at[ctx], me, block
        )

    for step in (2, 1, 3, 0):
        block = (ctx + step) % 4
        result = dot(upstream[...], w_out[at(block * COLS, COLS), :], NT).astype(BF16)
        if step == 0:
            gg_all[ctx] = result
        else:
            gg_send[block] = result
            gg_copy(block).start()
            sent.append(lambda block=block: gg_copy(block).wait_send())
            due["gg%d" % step] = lambda block=block: copy_to(gg_send.at[block], gg_all.at[block], gg_ssem.at[block], gg_rsem.at[block], me, block).wait_recv()

    def near_copy(p, side):
        rows = at(ctx * R + (plane + 4 - p) % 4 * 64, 64)
        return copy_to(
            normed.at[rows, :], normed.at[rows, :], z_send.at[side, p], z_recv.at[side, p], me, right if side == 0 else left
        )

    def near_arrival(p, side):
        rows = at((left if side == 0 else right) * R + (plane + 4 - p) % 4 * 64, 64)
        return copy_to(
            normed.at[rows, :], normed.at[rows, :], z_send.at[side, p], z_recv.at[side, p], me, right if side == 0 else left
        )

    def far_copy(p, side):
        rows = at((left if side == 0 else right) * R + (plane + 4 - p) % 4 * 64, 64)
        return copy_to(
            normed.at[rows, :], normed.at[rows, :], f_send.at[p], f_recv.at[p], me, right if side == 0 else left
        )

    def far_arrival(p, side):
        rows = at(far * R + (plane + 4 - p) % 4 * 64, 64)
        return copy_to(
            normed.at[rows, :], normed.at[rows, :], f_send.at[p], f_recv.at[p], me, right if side == 0 else left
        )

    for order, p in enumerate(PLANES):
        source = (plane + 4 - p) % 4

        @pl.loop(1 if p == 0 else 0, 8)
        def _(q):
            token_arrival(source * 8 + (inner + 8 - q) % 8).wait_recv()

        if order + AHEAD < 4:
            send_plane(PLANES[order + AHEAD])
        rows = join_halves(balanced[at(source * 128, 128), :].astype(F32))
        mean = jnp.mean(rows, axis=1, keepdims=True)
        centered = rows - mean
        inverse = lax.rsqrt(jnp.mean(centered * centered, axis=1, keepdims=True) + EPSILON)
        values = centered * inverse
        unit[at(source * 64, 64), :] = values
        inverse_in[at(source * 64, 64), :] = jnp.broadcast_to(inverse, (64, 128))
        normed[at(ctx * R + source * 64, 64), :] = values.astype(BF16)
        for side in range(2):
            near_copy(p, side).start()
            sent.append(lambda p=p, side=side: near_copy(p, side).wait_send())
            due["n%d%d" % (p, side)] = lambda p=p, side=side: near_arrival(p, side).wait_recv()

    for part in range(4):
        take("w%d" % part)

    attended[...] = jnp.zeros((LEN, COLS), F32)
    dq[...] = jnp.zeros((LEN, COLS), F32)
    dk[...] = jnp.zeros((LEN, COLS), F32)
    dv[...] = jnp.zeros((LEN, COLS), F32)
    bias_sum[...] = jnp.zeros((6, R, R), F32)

    end_0 = lengths[0, 0]
    end_1 = end_0 + lengths[0, 1]
    position = lax.broadcasted_iota(jnp.int32, (LEN, DH), 0)
    user = jnp.where(position >= end_0, 1, 0) + jnp.where(position >= end_1, 1, 0)
    same = user == lax.broadcasted_iota(jnp.int32, (LEN, DH), 1)
    q_user[...] = jnp.where(same, 1.0, 0.0).astype(BF16)
    k_user[...] = jnp.where(same, 0.0, HIDDEN).astype(BF16)

    def project(block):
        rows = at(block * R, R)
        for part in range(4):
            active, rate = silu_parts(0.5 * dot(normed[rows, :], w_in[:, part * COLS : part * COLS + COLS], NN))
            act[part, rows, :] = active.astype(BF16)
            slope[part, rows, :] = rate

    for p in PLANES[:2]:
        take("n%d%d" % (p, 0))
        far_copy(p, 0).start()
        sent.append(lambda p=p: far_copy(p, 0).wait_send())
        due["f%d%d" % (p, 0)] = lambda p=p: far_arrival(p, 0).wait_recv()

    for hh in range(HEADS):
        for r in range(3):
            reach = (
                lax.broadcasted_iota(jnp.int32, (R, R), 0) - lax.broadcasted_iota(jnp.int32, (R, R), 1) + (r * R + 1)
            )
            low, high = ((0, 8), (1, 9), (8, 9))[r]
            tile = jnp.full((R, R), 0.5 * bias_table[ctx * HEADS + hh, low], F32)
            for level in range(low + 1, high + 1):
                tile = jnp.where(reach >= 2**level, 0.5 * bias_table[ctx * HEADS + hh, level], tile)
            if r == 0:
                tile = jnp.where(reach >= 1, tile, HIDDEN)
            bias_tile[hh * 3 + r] = tile

    def pairs(place, body):
        @pl.loop(0, place + 1)
        def _(other):
            a = ordered[place]
            b = (ctx + other + other // 2 - 2 * (other // 3)) % 4
            a_last = (a - b + 4) // 4
            q = b + (a - b) * a_last
            k = a + b - q
            r = q - k

            @pl.when(r < 3)
            def _():
                body(q, k, r, q + 3 * r - r // 2)

    def attend(q, k, r, slot):
        q_rows, k_rows = at(q * R, R), at(k * R, R)
        for hh in range(HEADS):
            cols = slice(hh * DH, hh * DH + DH)
            query = jnp.concatenate((act[2, q_rows, cols], q_user[q_rows, :]), axis=1)
            keys = jnp.concatenate((act[3, k_rows, cols], k_user[k_rows, :]), axis=1)
            active, rate = silu_parts(dot(query, keys, NT) * (0.5 * SCALE) + bias_tile[hh * 3 + r])
            weights = active.astype(BF16)
            s_tile[hh, slot] = rate
            w_tile[hh, slot] = weights
            attended[q_rows, cols] += dot(weights, act[1, k_rows, cols], NN)

    project(ctx)
    for p in PLANES[2:]:
        take("n%d%d" % (p, 1))
        far_copy(p, 1).start()
        sent.append(lambda p=p: far_copy(p, 1).wait_send())
        due["f%d%d" % (p, 1)] = lambda p=p: far_arrival(p, 1).wait_recv()
    pairs(0, attend)
    for p in PLANES[:2]:
        take("n%d%d" % (p, 1))
    project(right)
    pairs(1, attend)
    for p in PLANES[2:]:
        take("n%d%d" % (p, 0))
    project(left)
    pairs(2, attend)
    for order, p in enumerate(PLANES):
        take("f%d%d" % (p, order // 2))
    project(far)
    pairs(3, attend)

    for step in range(1, 4):
        take("gg%d" % step)

    lane = lax.broadcasted_iota(jnp.int32, (R, 128), 1)

    @pl.loop(0, 4)
    def _(block):
        rows = attended[at(block * R, R), :]
        mean = jnp.mean(rows, axis=1, keepdims=True)
        centered = rows - mean
        flow = gg_all[block].astype(F32) * act[0, at(block * R, R), :].astype(F32)
        packed = jnp.where(lane == 0, mean, 0.0)
        packed = jnp.where(lane == 1, jnp.sum(centered * centered, axis=1, keepdims=True), packed)
        packed = jnp.where(lane == 2, jnp.sum(flow, axis=1, keepdims=True), packed)
        packed = jnp.where(lane == 3, jnp.sum(flow * centered, axis=1, keepdims=True), packed)
        stats_send[block] = packed.T[:8, :]

    def stats_copy(block):
        return copy_to(stats_send, stats_all.at[ctx], st_send.at[block], st_recv.at[ctx], me, block)

    for step in range(1, 4):
        stats_copy((ctx + step) % 4).start()
    stats_all[ctx] = stats_send[...]

    @pl.loop(0, 4)
    def _(piece):
        columns = at(piece * R, R)
        for b in range(4):
            turned[columns, b * R : b * R + R] = normed[b * R : b * R + R, columns].T

    for step in range(1, 4):
        block = (ctx + step) % 4
        sent.append(lambda block=block: stats_copy(block).wait_send())
        copy_to(stats_send, stats_all.at[block], st_send.at[block], st_recv.at[block], me, block).wait_recv()

    for block in range(4):
        parts = [stats_all[c, block] for c in range(4)]
        means = [x[0:1] for x in parts]
        mean = (means[0] + means[1] + means[2] + means[3]) * 0.25
        square = sum(parts[c][1:2] + COLS * (means[c] - mean) * (means[c] - mean) for c in range(4))
        flow = sum(parts[c][2:3] for c in range(4))
        cross = sum(parts[c][3:4] + (means[c] - mean) * parts[c][2:3] for c in range(4))
        inverse = lax.rsqrt(square * (1.0 / D) + EPSILON)
        table = jnp.concatenate(
            (mean, inverse, flow * (1.0 / D), cross * inverse * (1.0 / D), jnp.zeros((124, R), F32)), axis=0
        )
        rows_stat[pl.ds(block * R, R), :] = table.T

    def gated_copy(block):
        return copy_to(gated.at[block], gated_all.at[ctx], gt_send.at[block], gt_recv.at[ctx], me, block)

    @pl.loop(0, 4)
    def _(block):
        rows = at(block * R, R)
        table = rows_stat[rows, :]
        inverse = table[:, 1:2]
        out_unit = (attended[rows, :] - table[:, 0:1]) * inverse
        gate = act[0, rows, :].astype(F32)
        flow = gg_all[block].astype(F32)
        gated[block] = (out_unit * gate).astype(BF16)
        pg[rows, 0:COLS] = (flow * out_unit * slope[0, rows, :]).astype(BF16)
        att_grad[rows, :] = (inverse * (flow * gate - table[:, 2:3] - out_unit * table[:, 3:4])).astype(BF16)

    for step in range(1, 4):
        block = (ctx + step) % 4
        gated_copy(block).start()
        sent.append(lambda block=block: gated_copy(block).wait_send())
        due["gt%d" % step] = lambda block=block: copy_to(gated.at[block], gated_all.at[block], gt_send.at[block], gt_recv.at[block], me, block).wait_recv()
    gated_all[ctx] = gated[ctx]

    def core_copy(which, piece, half):
        cols = pl.ds(half * 512, 512)
        return copy_to(
            g_core.at[which, 1 - core, piece, :, cols], g_core_in.at[which, piece, :, cols], gc_send.at[which, piece, half],
            gc_recv.at[which, piece, half], partner, ctx,
        )

    def along_x(which, other):
        return copy_to(
            ga.at[which, other], ga_in.at[which, x], ga_send.at[which, other], ga_recv.at[which, x],
            (other * 4 + y) * 2 + core, ctx,
        )

    def from_x(which, other):
        return copy_to(
            ga.at[which, other], ga_in.at[which, other], ga_send.at[which, other], ga_recv.at[which, other],
            (other * 4 + y) * 2 + core, ctx,
        )

    def along_y(which, other):
        return copy_to(
            gb.at[which, other], gb_in.at[which, y], gb_send.at[which, other], gb_recv.at[which, y],
            (x * 4 + other) * 2 + core, ctx,
        )

    def from_y(which, other):
        return copy_to(
            gb.at[which, other], gb_in.at[which, other], gb_send.at[which, other], gb_recv.at[which, other],
            (x * 4 + other) * 2 + core, ctx,
        )

    def then_y(which, other):
        return copy_to(
            ha.at[which, other], ha_in.at[which, y], ha_send.at[which, other], ha_recv.at[which, y],
            (x * 4 + other) * 2 + core, ctx,
        )

    def then_from_y(which, other):
        return copy_to(
            ha.at[which, other], ha_in.at[which, other], ha_send.at[which, other], ha_recv.at[which, other],
            (x * 4 + other) * 2 + core, ctx,
        )

    def then_x(which, other):
        return copy_to(
            hb.at[which, other], hb_in.at[which, x], hb_send.at[which, other], hb_recv.at[which, x],
            (other * 4 + y) * 2 + core, ctx,
        )

    def then_from_x(which, other):
        return copy_to(
            hb.at[which, other], hb_in.at[which, other], hb_send.at[which, other], hb_recv.at[which, other],
            (other * 4 + y) * 2 + core, ctx,
        )

    def row_copy(which, block):
        return copy_to(
            g_row.at[which, at(block * 8, 8), :], g_row_in.at[which, ctx], gr_send.at[which, block],
            gr_recv.at[which, ctx], me, block,
        )

    def row_arrival(which, block):
        return copy_to(
            g_row.at[which, at(block * 8, 8), :], g_row_in.at[which, block], gr_send.at[which, block],
            gr_recv.at[which, block], me, block,
        )

    def keep_tile(which, piece, column, tile):
        halves = tile.reshape(4, 2, 32, COLS)
        first, second = halves[:, 0].reshape(128, COLS), halves[:, 1].reshape(128, COLS)
        cols = slice(column * COLS, column * COLS + COLS)
        g_core[which, 0, piece, :, cols] = first.astype(BF16)
        g_core[which, 1, piece, :, cols] = second.astype(BF16)

    def send_core(which, piece, half):
        core_copy(which, piece, half).start()
        sent.append(lambda: core_copy(which, piece, half).wait_send())
        due["gc%d%d%d" % (which, piece, half)] = lambda: core_copy(which, piece, half).wait_recv()

    def spread(which, half):
        cols = slice(half * 512, half * 512 + 512)
        for piece in range(4):
            take("gc%d%d%d" % (which, piece, half))
            both = g_core[which, core, piece, :, cols].astype(F32) + g_core_in[which, piece, :, cols].astype(F32)
            both = both.astype(BF16)
            if half == 0:
                ga[which, piece] = both.reshape(4, 32, 512)
            else:
                for row in range(4):
                    gb[which, row, piece] = both[row * 32 : row * 32 + 32]
        go, come, here = ((along_x, from_x, x), (along_y, from_y, y))[half]
        for step in (2, 1, 3):
            other = (here + step) % 4
            go(which, other).start()
            sent.append(lambda other=other: go(which, other).wait_send())
            due["g%d%d%d" % (half, which, step)] = lambda other=other: come(which, other).wait_recv()
        if half == 0:
            ga_in[which, x] = ga[which, x]
        else:
            gb_in[which, y] = gb[which, y]

    def spread_again(which, half):
        for step in (1, 3, 2):
            take("g%d%d%d" % (half, which, step))
        arrived, held, landed = ((ga_in, ha, ha_in), (gb_in, hb, hb_in))[half]
        total = arrived[which, 0].astype(F32)
        for other in range(1, 4):
            total = total + arrived[which, other].astype(F32)
        held[which] = total.astype(BF16)
        go, come, here = ((then_y, then_from_y, y), (then_x, then_from_x, x))[half]
        for step in (2, 1, 3):
            other = (here + step) % 4
            go(which, other).start()
            sent.append(lambda other=other: go(which, other).wait_send())
            due["h%d%d%d" % (half, which, step)] = lambda other=other: come(which, other).wait_recv()
        landed[which, here] = held[which, here]

    def finish_sum(which):
        for half in range(2):
            for step in (1, 3, 2):
                take("h%d%d%d" % (half, which, step))
            landed = (ha_in, hb_in)[half]
            total = landed[which, 0].astype(F32)
            for other in range(1, 4):
                total = total + landed[which, other].astype(F32)
            g_row[which, :, half * 512 : half * 512 + 512] = total
        for step in (2, 1, 3):
            block = (ctx + step) % 4
            row_copy(which, block).start()
            sent.append(lambda block=block: row_copy(which, block).wait_send())
            due["gr%d%d" % (which, step)] = lambda block=block: row_arrival(which, block).wait_recv()
        g_row_in[which, ctx] = g_row[which, at(ctx * 8, 8), :]

    def attend_back(q, k, r, slot):
        q_rows, k_rows = at(q * R, R), at(k * R, R)
        for hh in range(HEADS):
            cols = slice(hh * DH, hh * DH + DH)
            incoming = att_grad[q_rows, cols]
            change = dot(incoming, act[1, k_rows, cols], NT) * s_tile[hh, slot]
            bias_sum[hh * 3 + r] += change
            rounded = change.astype(BF16)
            dq[q_rows, cols] += dot(rounded, act[3, k_rows, cols], NN)
            dk[k_rows, cols] += dot(rounded, act[2, q_rows, cols], TN)
            dv[k_rows, cols] += dot(w_tile[hh, slot], incoming, TN)

    def close_block(block):
        rows = at(block * R, R)
        pg[rows, 1 * COLS : 1 * COLS + COLS] = (dv[rows, :] * slope[1, rows, :]).astype(BF16)
        pg[rows, 2 * COLS : 2 * COLS + COLS] = (dq[rows, :] * SCALE * slope[2, rows, :]).astype(BF16)
        pg[rows, 3 * COLS : 3 * COLS + COLS] = (dk[rows, :] * SCALE * slope[3, rows, :]).astype(BF16)

    def block_terms(block, half):
        rows = at(block * R, R)
        return dot(pg[rows, :], w_in[half * 512 : half * 512 + 512, :], NT)

    def far_part(side):
        return copy_to(
            ng_far.at[side], ng_far_in.at[side], nf_send.at[side], nf_recv.at[side], me, right if side == 0 else left
        )

    def near_part(side, half, p):
        rows = at((plane + p) % 4 * 64, 64)
        return copy_to(
            ng_near.at[side, half, rows, :], ng_near_in.at[side, half, rows, :], nn_send.at[side, half, p],
            nn_recv.at[side, half, p], me, right if side == 0 else left,
        )

    def send_near(side, half, p):
        near_part(side, half, p).start()
        sent.append(lambda: near_part(side, half, p).wait_send())
        due["nn%d%d%d" % (side, half, p)] = lambda: near_part(side, half, p).wait_recv()

    pairs(3, attend_back)
    close_block(far)
    for side in range(2):
        ng_far[side] = block_terms(far, side).astype(BF16)
        far_part(side).start()
        sent.append(lambda side=side: far_part(side).wait_send())
        due["nf%d" % side] = lambda side=side: far_part(side).wait_recv()

    for step in range(1, 4):
        take("gt%d" % step)
    for piece in range(4):
        left_rows = gated_all[piece].T

        for column in range(4):
            keep_tile(1, piece, column, dot(left_rows, upstream[:, column * COLS : column * COLS + COLS], NN))

        send_core(1, piece, 0)
        send_core(1, piece, 1)

    for place, side in ((2, 1), (1, 0)):
        pairs(place, attend_back)
        block = ordered[place]
        close_block(block)
        ng_near[side, 1 - side] = block_terms(block, 1 - side).astype(BF16)
        for p in PLANES:
            send_near(side, 1 - side, p)
    spread(1, 0)
    spread(1, 1)
    pairs(0, attend_back)
    close_block(ctx)

    def input_half(half):
        for piece in range(4):
            for part in range(half * 2, half * 2 + 2):
                cols = slice(part * COLS, part * COLS + COLS)
                keep_tile(0, piece, part, dot(turned[piece * R : piece * R + R, :], pg[:, cols], NN))

            send_core(0, piece, half)

    input_half(0)
    for side in range(2):
        terms = block_terms(right if side == 0 else left, side)
        take("nf%d" % side)
        ng_near[side, side] = (terms + ng_far_in[side].astype(F32)).astype(BF16)
    for p in PLANES:
        for side in range(2):
            send_near(side, side, p)
    spread(0, 0)
    input_half(1)
    spread_again(1, 0)
    spread_again(1, 1)
    spread(0, 1)
    for half in range(2):
        ng_own[:, half * 512 : half * 512 + 512] = block_terms(ctx, half)

    for half in range(2):
        cols = slice(half * 512, half * 512 + 512)
        total = dot(gated_all[0], w_out[0:COLS, cols], NN)
        for c in range(1, 4):
            total = total + dot(gated_all[c], w_out[c * COLS : c * COLS + COLS, cols], NN)
        pairs = balanced[...].astype(F32).reshape(32, 2, 8, 512)
        layer_output[:, cols] = (pairs[:, half].reshape(R, 512) + total).astype(BF16)

    sums = jnp.zeros((8, 128), F32)
    tile_row = lax.broadcasted_iota(jnp.int32, (8, 128), 0)
    tile_lane = lax.broadcasted_iota(jnp.int32, (8, 128), 1)
    for hh in range(HEADS):
        for r in range(3):
            reach = (
                lax.broadcasted_iota(jnp.int32, (R, R), 0) - lax.broadcasted_iota(jnp.int32, (R, R), 1) + (r * R + 1)
            )
            low, high = ((0, 8), (1, 9), (8, 9))[r]
            tile = bias_sum[hh * 3 + r]
            for level in range(low, high + 1):
                part = tile
                if level > low:
                    part = jnp.where(reach >= 2**level, part, 0.0)
                if level < high:
                    part = jnp.where(reach < 2 ** (level + 1), part, 0.0)
                total = jnp.sum(jnp.sum(part, axis=0, keepdims=True), axis=1, keepdims=True)
                place = jnp.logical_and(tile_row == ctx * HEADS + hh, tile_lane == level)
                sums = sums + jnp.where(place, total, 0.0)
    b_core[...] = sums
    bias_core = copy_to(b_core, b_core_in, bc_send, bc_recv, partner, ctx)
    bias_core.start()
    sent.append(lambda: bias_core.wait_send())
    due["bc"] = lambda: bias_core.wait_recv()


    def back_copy(dst):
        return copy_to(
            back.at[at(dst * 16, 16), :], back_in.at[at(me * 16, 16), :], r_send.at[dst], r_recv.at[me], dst, ctx
        )

    def back_arrival(src):
        return copy_to(
            back.at[at(src * 16, 16), :], back_in.at[at(src * 16, 16), :], r_send.at[src], r_recv.at[src], src, ctx
        )

    for order, p in enumerate(PLANES):
        if order > 1:
            spread_again(0, order - 2)
        for side in range(2):
            for half in range(2):
                take("nn%d%d%d" % (side, half, p))
        target = (plane + p) % 4
        rows = at(target * 64, 64)
        total = []
        for half in range(2):
            total.append(
                ng_own[rows, half * 512 : half * 512 + 512]
                + ng_near_in[0, half, rows, :].astype(F32)
                + ng_near_in[1, half, rows, :].astype(F32)
            )
        total = jnp.concatenate(total, axis=1)
        values = unit[rows, :]
        plain = jnp.mean(total, axis=1, keepdims=True)
        cross = jnp.mean(total * values, axis=1, keepdims=True)
        change = inverse_in[rows, 0:1] * (total - plain - values * cross)
        result = upstream[rows, :].astype(F32) + change
        back[at(target * 128, 128), :] = split_halves(result).astype(BF16)

        @pl.loop(1 if p == 0 else 0, 8)
        def _(q):
            back_copy(target * 8 + (inner + q) % 8).start()

    back_in[at(me * 16, 16), :] = back[at(me * 16, 16), :]
    sent.append(lambda: ring(32, me, lambda o: back_copy(o).wait_send()))
    due["back"] = lambda: ring(32, me, lambda o: back_arrival(o).wait_recv())

    take("bc")
    b_chip_in[chip] = b_core[...] + b_core_in[...]

    def bias_chip(other):
        return copy_to(
            b_chip_in.at[chip], b_chip_in.at[chip], bk_send.at[other], bk_recv.at[chip], other * 2 + core, ctx
        )

    @pl.loop(1, 16)
    def _(step):
        bias_chip((chip + step) % 16).start()

    sent.append(lambda: ring(16, chip, lambda o: bias_chip(o).wait_send()))
    due["bk"] = lambda: ring(16, chip, lambda other: copy_to(
            b_chip_in.at[other], b_chip_in.at[other], bk_send.at[other], bk_recv.at[other], other * 2 + core, ctx
        ).wait_recv())
    finish_sum(1)
    finish_sum(0)
    take("bk")

    total = b_chip_in[0]
    for other in range(1, 16):
        total = total + b_chip_in[other]
    b_row[...] = total
    b_row_in[ctx] = total
    for step in range(1, 4):
        block = (ctx + step) % 4
        copy_to(b_row, b_row_in.at[ctx], br_send.at[block], br_recv.at[ctx], me, block).start()
        sent.append(lambda block=block: copy_to(b_row, b_row_in.at[ctx], br_send.at[block], br_recv.at[ctx], me, block).wait_send())

    take("back")

    returned = join_halves(back_in[...].astype(F32)).astype(BF16)
    token_gradient[...] = dot(pick[...], returned, NN).astype(BF16)

    for step in range(1, 4):
        block = (ctx + step) % 4
        take("gr0%d" % step)
        take("gr1%d" % step)
        copy_to(b_row, b_row_in.at[block], br_send.at[block], br_recv.at[block], me, block).wait_recv()
    for c in range(4):
        for part in range(4):
            input_gradient[:, part * D + c * COLS : part * D + c * COLS + COLS] = g_row_in[
                0, c, :, part * COLS : part * COLS + COLS
            ]
    output_gradient[...] = g_row_in[1, 0] + g_row_in[1, 1] + g_row_in[1, 2] + g_row_in[1, 3]
    bias_gradient[...] = (b_row_in[0] + b_row_in[1] + b_row_in[2] + b_row_in[3])[:, :NB]

    for fn in sent:
        fn()


def hand_over(*refs):
    for source, target in zip(refs[:5], refs[5:]):
        target[...] = source[...]


def shards(tokens, send_rows, user_lengths, input_weight, output_weight, distance_bias, upstream):
    vmem = pl.BlockSpec(memory_space=pltpu.VMEM)
    smem = pl.BlockSpec(memory_space=pltpu.SMEM)
    hbm = pl.BlockSpec(memory_space=pl.ANY)
    dma = pltpu.SemaphoreType.DMA
    V = pltpu.VMEM
    scratch = [
        V((D, D), BF16), V((D, D), BF16), V((R, R), BF16), V((512, 512), BF16), V((512, 512), BF16),
        V((R, D), F32), V((R, 128), F32), V((LEN, D), BF16), V((4, R, COLS), BF16), V((4, R, COLS), BF16),
        V((4, LEN, COLS), F32), V((4, LEN, COLS), BF16), V((6, R, R), F32),
        V((HEADS, 9, R, R), BF16), V((HEADS, 9, R, R), F32), V((LEN, COLS), F32),
        V((4, 8, R), F32), V((4, 4, 8, R), F32), V((LEN, 128), F32),
        V((4, R, COLS), BF16), V((4, R, COLS), BF16), V((LEN, COLS), BF16),
        V((LEN, COLS), F32), V((LEN, COLS), F32), V((LEN, COLS), F32), V((6, R, R), F32), V((LEN, D), BF16), V((D, LEN), BF16),
        V((LEN, DH), BF16), V((LEN, DH), BF16),
        V((2, R, 512), BF16), V((2, R, 512), BF16), V((2, 2, R, 512), BF16), V((2, 2, R, 512), BF16), V((R, D), F32),
        V((512, 512), BF16), V((512, 512), BF16),
        V((2, 2, 4, 128, D), BF16), V((2, 4, 128, D), BF16),
        V((2, 4, 4, 32, 512), BF16), V((2, 4, 4, 32, 512), BF16), V((2, 4, 4, 32, 512), BF16),
        V((2, 4, 4, 32, 512), BF16), V((2, 4, 32, 512), BF16), V((2, 4, 32, 512), BF16),
        V((2, 4, 32, 512), BF16), V((2, 4, 32, 512), BF16), V((2, 32, D), F32), V((2, 4, 8, D), F32),
        V((8, 128), F32), V((8, 128), F32), V((16, 8, 128), F32), V((8, 128), F32), V((4, 8, 128), F32),
        dma((5,)), dma((32,)), dma((32,)), dma((4,)), dma((4,)), dma((2, 4)), dma((2, 4)), dma((4,)), dma((4,)),
        dma((4,)), dma((4,)), dma((4,)), dma((4,)),
        dma((2,)), dma((2,)), dma((2, 2, 4)), dma((2, 2, 4)), dma((32,)), dma((32,)),
        dma((2, 4, 2)), dma((2, 4, 2)), dma((2, 4)), dma((2, 4)), dma((2, 4)), dma((2, 4)), dma((2, 4)), dma((2, 4)),
        dma((2, 4)), dma((2, 4)), dma((2, 4)), dma((2, 4)),
        dma(()), dma(()), dma((16,)), dma((16,)), dma((4,)), dma((4,)),
    ]
    outs = pl.pallas_call(
        kernel,
        out_shape=(
            jax.ShapeDtypeStruct((R, D), BF16),
            jax.ShapeDtypeStruct((R, D), BF16),
            jax.ShapeDtypeStruct((8, 4 * D), F32),
            jax.ShapeDtypeStruct((8, D), F32),
            jax.ShapeDtypeStruct((8, NB), F32),
        ),
        in_specs=[vmem, vmem, smem, hbm, hbm, smem, vmem],
        out_specs=(vmem,) * 5,
        scratch_shapes=scratch,
        compiler_params=pltpu.CompilerParams(
            collective_id=0, has_side_effects=True, vmem_limit_bytes=60 * 1024 * 1024
        ),
        name="hstu_layer",
    )(tokens, send_rows, user_lengths, input_weight, output_weight, distance_bias, upstream)
    return pl.pallas_call(
        hand_over,
        out_shape=tuple(jax.ShapeDtypeStruct(o.shape, o.dtype) for o in outs),
        in_specs=[vmem] * 5,
        out_specs=(vmem,) * 5,
        name="results",
    )(*outs)


def solution(mesh):
    block = P(("dp", "ctx"), None)
    in_specs = (block, block, P("dp", None), P(), P(), P(), block)
    out_specs = (block, block, block, block, P())
    return jax.shard_map(shards, mesh=mesh, in_specs=in_specs, out_specs=out_specs, check_vma=False)
```

time: 124 us -> 98.4 us (0.79)
  the two profiles are of different devices: /device:TPU:4 before, /device:TPU:0 now
where the time goes in v3:
time: 98.4 us; the launch traced here: 97.9 us
  Pallas kernels  97.3 us (99%)
    pallas_call x1, Pallas kernels, shards(): pl.pallas_call(kernel, out_shape=(jax.ShapeDtypeStruct((R, D), BF16), jax...  95 us
    pallas_call x1, Pallas kernels, shards(): pl.pallas_call(hand_over, out_shape=tuple((jax.ShapeDtypeStruct(o.shape,...  2.29 us

profile of v3, /device:TPU:0, one launch (start us, length us, event | category | flops | bytes accessed | tf_op | source)
XLA Modules:
  0.0 97.9 jit_solution(10569143770042787190)
XLA Ops:
  0.6 95.0 %hstu_layer.1 = (bf16[256,1024]{1,0:T(8,128)(2,1)}, bf16[256,1024]{1,0:T(8,128)(2,1)}, f32[8,4096]{1,0:T(8,128)}, f32[8,1024]{1,0:T(8,128)}, f32[8,12]{1,0:T(8,128)}) custom-call(bf16[256,1024]{1,0:T(8,128)(2,1)} %tokens.1, s32[1,256]{1,0:T(1,128)} %send_rows.1, s32[1,3]{1,0:T(1,128)} %lengths.1, bf16[1024,4096]{1,0:T(8,128)(2,1)} %weight_in.1, ...), custom_call_target="tpu_custom_call" | custom-call | tf_op jit(solution)/shard_map/hstu_layer/pallas_call | solution.py:749
  95.6 2.3 %results.1 = (bf16[256,1024]{1,0:T(8,128)(2,1)}, bf16[256,1024]{1,0:T(8,128)(2,1)}, f32[8,4096]{1,0:T(8,128)}, f32[8,1024]{1,0:T(8,128)}, f32[8,12]{1,0:T(8,128)}) custom-call(bf16[256,1024]{1,0:T(8,128)(2,1)} %get-tuple-element.10.refs_0_, bf16[256,1024]{1,0:T(8,128)(2,1)} %get-tuple-element.11.refs_1_, f32[8,4096]{1,0:T(8,128)} %get-tuple-element.12.refs_2_, ...), custom_call_target="tpu_custom_call" | custom-call | tf_op jit(solution)/shard_map/results/pallas_call | solution.py:766

commit v4 on v3

--- a/solution.py
+++ b/solution.py
@@ -39,7 +39,8 @@
 def silu_parts(halved):
     rise = 1.0 + jnp.tanh(halved)
     active = halved * rise
-    return active, active + (0.5 * rise) * (1.0 - active)
+    gate = 0.5 * rise
+    return active, gate + active * (1.0 - gate)
 
 
 def copy_to(src, dst, send_sem, recv_sem, dp, ctx):
@@ -89,6 +90,15 @@
     x, y = chip // 4, chip % 4
     ordered = (ctx, right, left, far)
 
+    barrier = pltpu.get_barrier_semaphore()
+
+    @pl.loop(1, 32)
+    def _(step):
+        pl.semaphore_signal(barrier, inc=1, device_id=((me + step) % 32, ctx), device_id_type=MESH)
+
+    for step in range(1, 4):
+        pl.semaphore_signal(barrier, inc=1, device_id=(me, (ctx + step) % 4), device_id_type=MESH)
+
     out_copy = pltpu.make_async_copy(weight_out, w_out, w_sem.at[4])
     out_copy.start()
     in_copies = []
@@ -100,18 +110,19 @@
     for part in range(4):
         due["w%d" % part] = in_copies[part].wait
 
-    barrier = pltpu.get_barrier_semaphore()
-
-    @pl.loop(1, 32)
-    def _(step):
-        pl.semaphore_signal(barrier, inc=1, device_id=((me + step) % 32, ctx), device_id_type=MESH)
-
-    for step in range(1, 4):
-        pl.semaphore_signal(barrier, inc=1, device_id=(me, (ctx + step) % 4), device_id_type=MESH)
-
     rows_of = lax.broadcasted_iota(jnp.int32, (R, R), 0)
     pick[...] = jnp.where(rows_of == send_rows[...], 1.0, 0.0).astype(BF16)
     message[...] = split_halves(dot(pick[...], tokens[...], TN)).astype(BF16)
+
+    take("w4")
+
+    def gg_copy(block):
+        return copy_to(
+            gg_send.at[block], gg_all.at[ctx], gg_ssem.at[block], gg_rsem.at[ctx], me, block
+        )
+
+    for block in range(4):
+        gg_send[block] = dot(upstream[...], w_out[block * COLS : block * COLS + COLS, :], NT).astype(BF16)
 
     pl.semaphore_wait(barrier, 34)
 
@@ -135,23 +146,14 @@
     balanced[at(me * 16, 16), :] = message[at(me * 16, 16), :]
     sent.append(lambda: ring(32, me, lambda o: token_copy(o).wait_send()))
 
-    take("w4")
-
-    def gg_copy(block):
-        return copy_to(
-            gg_send.at[block], gg_all.at[ctx], gg_ssem.at[block], gg_rsem.at[ctx], me, block
-        )
-
-    for step in (2, 1, 3, 0):
+    for step in (2, 1, 3):
         block = (ctx + step) % 4
-        result = dot(upstream[...], w_out[at(block * COLS, COLS), :], NT).astype(BF16)
-        if step == 0:
-            gg_all[ctx] = result
-        else:
-            gg_send[block] = result
-            gg_copy(block).start()
-            sent.append(lambda block=block: gg_copy(block).wait_send())
-            due["gg%d" % step] = lambda block=block: copy_to(gg_send.at[block], gg_all.at[block], gg_ssem.at[block], gg_rsem.at[block], me, block).wait_recv()
+        gg_copy(block).start()
+        sent.append(lambda block=block: gg_copy(block).wait_send())
+        due["gg%d" % step] = lambda block=block: copy_to(
+            gg_send.at[block], gg_all.at[block], gg_ssem.at[block], gg_rsem.at[block], me, block
+        ).wait_recv()
+    gg_all[ctx] = gg_send[ctx]
 
     def near_copy(p, side):
         rows = at(ctx * R + (plane + 4 - p) % 4 * 64, 64)
@@ -218,10 +220,12 @@
 
     def project(block):
         rows = at(block * R, R)
-        for part in range(4):
-            active, rate = silu_parts(0.5 * dot(normed[rows, :], w_in[:, part * COLS : part * COLS + COLS], NN))
-            act[part, rows, :] = active.astype(BF16)
-            slope[part, rows, :] = rate
+        for half in range(2):
+            active, rate = silu_parts(0.5 * dot(normed[rows, :], w_in[:, half * 512 : half * 512 + 512], NN))
+            for part in range(2):
+                cols = slice(part * COLS, part * COLS + COLS)
+                act[half * 2 + part, rows, :] = active[:, cols].astype(BF16)
+                slope[half * 2 + part, rows, :] = rate[:, cols]
 
     for p in PLANES[:2]:
         take("n%d%d" % (p, 0))
@@ -377,16 +381,16 @@
             (other * 4 + y) * 2 + core, ctx,
         )
 
-    def along_y(which, other):
-        return copy_to(
-            gb.at[which, other], gb_in.at[which, y], gb_send.at[which, other], gb_recv.at[which, y],
-            (x * 4 + other) * 2 + core, ctx,
-        )
-
-    def from_y(which, other):
-        return copy_to(
-            gb.at[which, other], gb_in.at[which, other], gb_send.at[which, other], gb_recv.at[which, other],
-            (x * 4 + other) * 2 + core, ctx,
+    def along_y(which, other, piece):
+        return copy_to(
+            gb.at[which, other, piece], gb_in.at[which, y, piece], gb_send.at[which, other, piece],
+            gb_recv.at[which, y, piece], (x * 4 + other) * 2 + core, ctx,
+        )
+
+    def from_y(which, other, piece):
+        return copy_to(
+            gb.at[which, other, piece], gb_in.at[which, other, piece], gb_send.at[which, other, piece],
+            gb_recv.at[which, other, piece], (x * 4 + other) * 2 + core, ctx,
         )
 
     def then_y(which, other):
@@ -425,39 +429,52 @@
             gr_recv.at[which, block], me, block,
         )
 
-    def keep_tile(which, piece, column, tile):
-        halves = tile.reshape(4, 2, 32, COLS)
-        first, second = halves[:, 0].reshape(128, COLS), halves[:, 1].reshape(128, COLS)
-        cols = slice(column * COLS, column * COLS + COLS)
-        g_core[which, 0, piece, :, cols] = first.astype(BF16)
-        g_core[which, 1, piece, :, cols] = second.astype(BF16)
-
-    def send_core(which, piece, half):
+    def keep_half(which, piece, half, tile):
+        pairs_of = tile.reshape(4, 2, 32, 512)
+        cols = slice(half * 512, half * 512 + 512)
+        for own in range(2):
+            g_core[which, own, piece, :, cols] = pairs_of[:, own].reshape(128, 512).astype(BF16)
+
+    def send_core(which, place, piece, half):
         core_copy(which, piece, half).start()
         sent.append(lambda: core_copy(which, piece, half).wait_send())
-        due["gc%d%d%d" % (which, piece, half)] = lambda: core_copy(which, piece, half).wait_recv()
-
-    def spread(which, half):
+        due["gc%d%d%d" % (which, place, half)] = lambda: core_copy(which, piece, half).wait_recv()
+
+    def spread(which, place, piece, half):
         cols = slice(half * 512, half * 512 + 512)
-        for piece in range(4):
-            take("gc%d%d%d" % (which, piece, half))
-            both = g_core[which, core, piece, :, cols].astype(F32) + g_core_in[which, piece, :, cols].astype(F32)
-            both = both.astype(BF16)
-            if half == 0:
-                ga[which, piece] = both.reshape(4, 32, 512)
-            else:
-                for row in range(4):
-                    gb[which, row, piece] = both[row * 32 : row * 32 + 32]
-        go, come, here = ((along_x, from_x, x), (along_y, from_y, y))[half]
-        for step in (2, 1, 3):
-            other = (here + step) % 4
-            go(which, other).start()
-            sent.append(lambda other=other: go(which, other).wait_send())
-            due["g%d%d%d" % (half, which, step)] = lambda other=other: come(which, other).wait_recv()
+        take("gc%d%d%d" % (which, place, half))
+        both = g_core[which, core, piece, :, cols].astype(F32) + g_core_in[which, piece, :, cols].astype(F32)
+        both = both.astype(BF16)
         if half == 0:
-            ga_in[which, x] = ga[which, x]
+            ga[which, piece] = both.reshape(4, 32, 512)
+
+            @pl.when(piece != x)
+            def _():
+                along_x(which, piece).start()
+
+            @pl.when(piece == x)
+            def _():
+                ga_in[which, x] = ga[which, x]
+
         else:
-            gb_in[which, y] = gb[which, y]
+            for row in range(4):
+                gb[which, row, piece] = both[row * 32 : row * 32 + 32]
+            for step in (2, 1, 3):
+                other = (y + step) % 4
+                along_y(which, other, piece).start()
+                sent.append(lambda other=other: along_y(which, other, piece).wait_send())
+            gb_in[which, y, piece] = gb[which, y, piece]
+
+    def await_spread(which):
+        for step in range(1, 4):
+            sent.append(lambda other=(x + step) % 4: along_x(which, other).wait_send())
+            due["g0%d%d" % (which, step)] = lambda other=(x + step) % 4: from_x(which, other).wait_recv()
+
+            def wait_rows(other=(y + step) % 4):
+                for piece in range(4):
+                    from_y(which, other, piece).wait_recv()
+
+            due["g1%d%d" % (which, step)] = wait_rows
 
     def spread_again(which, half):
         for step in (1, 3, 2):
@@ -530,6 +547,8 @@
         sent.append(lambda: near_part(side, half, p).wait_send())
         due["nn%d%d%d" % (side, half, p)] = lambda: near_part(side, half, p).wait_recv()
 
+    await_spread(1)
+    await_spread(0)
     pairs(3, attend_back)
     close_block(far)
     for side in range(2):
@@ -538,17 +557,6 @@
         sent.append(lambda side=side: far_part(side).wait_send())
         due["nf%d" % side] = lambda side=side: far_part(side).wait_recv()
 
-    for step in range(1, 4):
-        take("gt%d" % step)
-    for piece in range(4):
-        left_rows = gated_all[piece].T
-
-        for column in range(4):
-            keep_tile(1, piece, column, dot(left_rows, upstream[:, column * COLS : column * COLS + COLS], NN))
-
-        send_core(1, piece, 0)
-        send_core(1, piece, 1)
-
     for place, side in ((2, 1), (1, 0)):
         pairs(place, attend_back)
         block = ordered[place]
@@ -556,20 +564,33 @@
         ng_near[side, 1 - side] = block_terms(block, 1 - side).astype(BF16)
         for p in PLANES:
             send_near(side, 1 - side, p)
-    spread(1, 0)
-    spread(1, 1)
     pairs(0, attend_back)
     close_block(ctx)
 
+    turn = [(x + step) % 4 for step in (2, 1, 3, 0)]
+    for step in range(1, 4):
+        take("gt%d" % step)
+    for place in range(4):
+        left_rows = gated_all[turn[place]].T
+        for half in range(2):
+            keep_half(1, turn[place], half, dot(left_rows, upstream[:, half * 512 : half * 512 + 512], NN))
+            send_core(1, place, turn[place], half)
+            if place > 1:
+                spread(1, place - 2, turn[place - 2], half)
+
     def input_half(half):
-        for piece in range(4):
-            for part in range(half * 2, half * 2 + 2):
-                cols = slice(part * COLS, part * COLS + COLS)
-                keep_tile(0, piece, part, dot(turned[piece * R : piece * R + R, :], pg[:, cols], NN))
-
-            send_core(0, piece, half)
-
-    input_half(0)
+        for place in range(4):
+            piece = turn[place]
+            keep_half(0, piece, half, dot(turned[at(piece * R, R), :], pg[:, half * 512 : half * 512 + 512], NN))
+            send_core(0, place, piece, half)
+            if place > 1:
+                spread(0, place - 2, turn[place - 2], half)
+        return lambda: [spread(0, place, turn[place], half) for place in (2, 3)]
+
+    rest = input_half(0)
+    for place in (2, 3):
+        for half in range(2):
+            spread(1, place, turn[place], half)
     for side in range(2):
         terms = block_terms(right if side == 0 else left, side)
         take("nf%d" % side)
@@ -577,21 +598,13 @@
     for p in PLANES:
         for side in range(2):
             send_near(side, side, p)
-    spread(0, 0)
-    input_half(1)
+    rest()
+    rest = input_half(1)
+    rest()
     spread_again(1, 0)
     spread_again(1, 1)
-    spread(0, 1)
     for half in range(2):
         ng_own[:, half * 512 : half * 512 + 512] = block_terms(ctx, half)
-
-    for half in range(2):
-        cols = slice(half * 512, half * 512 + 512)
-        total = dot(gated_all[0], w_out[0:COLS, cols], NN)
-        for c in range(1, 4):
-            total = total + dot(gated_all[c], w_out[c * COLS : c * COLS + COLS, cols], NN)
-        pairs = balanced[...].astype(F32).reshape(32, 2, 8, 512)
-        layer_output[:, cols] = (pairs[:, half].reshape(R, 512) + total).astype(BF16)
 
     sums = jnp.zeros((8, 128), F32)
     tile_row = lax.broadcasted_iota(jnp.int32, (8, 128), 0)
@@ -676,6 +689,14 @@
     due["bk"] = lambda: ring(16, chip, lambda other: copy_to(
             b_chip_in.at[other], b_chip_in.at[other], bk_send.at[other], bk_recv.at[other], other * 2 + core, ctx
         ).wait_recv())
+    for half in range(2):
+        cols = slice(half * 512, half * 512 + 512)
+        total = dot(gated_all[0], w_out[0:COLS, cols], NN)
+        for c in range(1, 4):
+            total = total + dot(gated_all[c], w_out[c * COLS : c * COLS + COLS, cols], NN)
+        pairs = balanced[...].astype(F32).reshape(32, 2, 8, 512)
+        layer_output[:, cols] = (pairs[:, half].reshape(R, 512) + total).astype(BF16)
+
     finish_sum(1)
     finish_sum(0)
     take("bk")
@@ -742,7 +763,7 @@
         dma((5,)), dma((32,)), dma((32,)), dma((4,)), dma((4,)), dma((2, 4)), dma((2, 4)), dma((4,)), dma((4,)),
         dma((4,)), dma((4,)), dma((4,)), dma((4,)),
         dma((2,)), dma((2,)), dma((2, 2, 4)), dma((2, 2, 4)), dma((32,)), dma((32,)),
-        dma((2, 4, 2)), dma((2, 4, 2)), dma((2, 4)), dma((2, 4)), dma((2, 4)), dma((2, 4)), dma((2, 4)), dma((2, 4)),
+        dma((2, 4, 2)), dma((2, 4, 2)), dma((2, 4)), dma((2, 4)), dma((2, 4, 4)), dma((2, 4, 4)), dma((2, 4)), dma((2, 4)),
         dma((2, 4)), dma((2, 4)), dma((2, 4)), dma((2, 4)),
         dma(()), dma(()), dma((16,)), dma((16,)), dma((4,)), dma((4,)),
     ]

time: 98.4 us -> 94 us (0.955)
  Pallas kernels: 97.3 us -> 93 us
    pallas_call x1, Pallas kernels: 95 us -> 90.7 us  [shards(): pl.pallas_call(kernel, out_shape=(jax.ShapeDtypeStruct((R, D), BF16), jax...]
where the time goes in v4:
time: 94 us; the launch traced here: 93.7 us
  Pallas kernels  93 us (99%)
    pallas_call x1, Pallas kernels, shards(): pl.pallas_call(kernel, out_shape=(jax.ShapeDtypeStruct((R, D), BF16), jax...  90.7 us
    pallas_call x1, Pallas kernels, shards(): pl.pallas_call(hand_over, out_shape=tuple((jax.ShapeDtypeStruct(o.shape,...  2.29 us

profile of v4, /device:TPU:0, one launch (start us, length us, event | category | flops | bytes accessed | tf_op | source)
XLA Modules:
  0.0 93.7 jit_solution(13974280536187527151)
XLA Ops:
  0.6 90.7 %hstu_layer.1 = (bf16[256,1024]{1,0:T(8,128)(2,1)}, bf16[256,1024]{1,0:T(8,128)(2,1)}, f32[8,4096]{1,0:T(8,128)}, f32[8,1024]{1,0:T(8,128)}, f32[8,12]{1,0:T(8,128)}) custom-call(bf16[256,1024]{1,0:T(8,128)(2,1)} %tokens.1, s32[1,256]{1,0:T(1,128)} %send_rows.1, s32[1,3]{1,0:T(1,128)} %lengths.1, bf16[1024,4096]{1,0:T(8,128)(2,1)} %weight_in.1, ...), custom_call_target="tpu_custom_call" | custom-call | tf_op jit(solution)/shard_map/hstu_layer/pallas_call | solution.py:770
  91.4 2.3 %results.1 = (bf16[256,1024]{1,0:T(8,128)(2,1)}, bf16[256,1024]{1,0:T(8,128)(2,1)}, f32[8,4096]{1,0:T(8,128)}, f32[8,1024]{1,0:T(8,128)}, f32[8,12]{1,0:T(8,128)}) custom-call(bf16[256,1024]{1,0:T(8,128)(2,1)} %get-tuple-element.10.refs_0_, bf16[256,1024]{1,0:T(8,128)(2,1)} %get-tuple-element.11.refs_1_, f32[8,4096]{1,0:T(8,128)} %get-tuple-element.12.refs_2_, ...), custom_call_target="tpu_custom_call" | custom-call | tf_op jit(solution)/shard_map/results/pallas_call | solution.py:787

commit v5 on v4

--- a/solution.py
+++ b/solution.py
@@ -643,8 +643,8 @@
         )
 
     for order, p in enumerate(PLANES):
-        if order > 1:
-            spread_again(0, order - 2)
+        if order < 2:
+            spread_again(0, order)
         for side in range(2):
             for half in range(2):
                 take("nn%d%d%d" % (side, half, p))

time: 94 us -> 94.8 us (level)
  Pallas kernels: 93 us -> 94 us
    pallas_call x1, Pallas kernels: 90.7 us -> 91.7 us  [shards(): pl.pallas_call(kernel, out_shape=(jax.ShapeDtypeStruct((R, D), BF16), jax...]
where the time goes in v5:
time: 94.8 us; the launch traced here: 94.6 us
  Pallas kernels  94 us (99%)
    pallas_call x1, Pallas kernels, shards(): pl.pallas_call(kernel, out_shape=(jax.ShapeDtypeStruct((R, D), BF16), jax...  91.7 us
    pallas_call x1, Pallas kernels, shards(): pl.pallas_call(hand_over, out_shape=tuple((jax.ShapeDtypeStruct(o.shape,...  2.29 us

profile of v5, /device:TPU:0, one launch (start us, length us, event | category | flops | bytes accessed | tf_op | source)
XLA Modules:
  0.0 94.6 jit_solution(8943629287266291140)
XLA Ops:
  0.6 91.7 %hstu_layer.1 = (bf16[256,1024]{1,0:T(8,128)(2,1)}, bf16[256,1024]{1,0:T(8,128)(2,1)}, f32[8,4096]{1,0:T(8,128)}, f32[8,1024]{1,0:T(8,128)}, f32[8,12]{1,0:T(8,128)}) custom-call(bf16[256,1024]{1,0:T(8,128)(2,1)} %tokens.1, s32[1,256]{1,0:T(1,128)} %send_rows.1, s32[1,3]{1,0:T(1,128)} %lengths.1, bf16[1024,4096]{1,0:T(8,128)(2,1)} %weight_in.1, ...), custom_call_target="tpu_custom_call" | custom-call | tf_op jit(solution)/shard_map/hstu_layer/pallas_call | solution.py:770
  92.3 2.3 %results.1 = (bf16[256,1024]{1,0:T(8,128)(2,1)}, bf16[256,1024]{1,0:T(8,128)(2,1)}, f32[8,4096]{1,0:T(8,128)}, f32[8,1024]{1,0:T(8,128)}, f32[8,12]{1,0:T(8,128)}) custom-call(bf16[256,1024]{1,0:T(8,128)(2,1)} %get-tuple-element.10.refs_0_, bf16[256,1024]{1,0:T(8,128)(2,1)} %get-tuple-element.11.refs_1_, f32[8,4096]{1,0:T(8,128)} %get-tuple-element.12.refs_2_, ...), custom_call_target="tpu_custom_call" | custom-call | tf_op jit(solution)/shard_map/results/pallas_call | solution.py:787
